TPU v7x, 256 devices: a whole 4x4x8 slice. The times are simulated.
256 devices in a mesh: dp: 8 (over z), section: 4 (over y), mp: 8 (over x, core).
Axes of the slice: x: 4, y: 4, z: 8, core: 2. Of those that a mesh axis runs over, the one named last changes fastest.
Arguments:
- patches: bfloat16 [1, 8192, 1280], P(None, ('dp', 'mp')), may hold values from -6 to 6
- windows: int32 [1, 8192], P(None, ('dp', 'mp')), may hold values from 0 to 8191, as said below
- gain: float32 [4, 1280], P('section'), may hold values from 0.25 to 1.75
- w_qkv: bfloat16 [4, 1280, 1920], P('section'), may hold values from -3 to 3
- w_out: bfloat16 [4, 640, 1280], P('section'), may hold values from -0.25 to 0.25
- cotangent: bfloat16 [1, 8192, 1280], P(None, ('dp', 'mp')), may hold values from -16 to 16
Outputs:
- activations: bfloat16 [4, 1, 8192, 1280], P('section', None, ('dp', 'mp'))
- input_grads: bfloat16 [4, 1, 8192, 1280], P('section', None, ('dp', 'mp'))
- grad_qkv: float32 [4, 1280, 1920], P('section', ('dp', 'mp'))
- grad_out: float32 [4, 640, 1280], P('section', None, ('dp', 'mp'))
- grad_gain: float32 [4, 1280], P('section', ('dp', 'mp'))
Inputs may be any that keep to these rules, and one draw needn't show every extreme that they name: `windows`: A window's number is the index of its first patch among all patches of all micro-batches laid end to end, so numbers never fall; a window's patches are consecutive and lie inside one aligned block of 128 patches; every window holds 1 to 112 patches, and every block holds one window of exactly 112.
All inputs are finite; a program needn't handle non-finite values.
Results may differ from a plain program's by a relative error of at most 0.025.
Values may be sent and summed in bfloat16 or wider, within the bound.
A program may use at most 192 MiB of HBM per device.

v0:
```python
import jax
import jax.numpy as jnp
from jax import lax
from jax.sharding import PartitionSpec as P

HEAD = 80


def from_behind(x, axis, by):
    peers = lax.axis_size(axis)
    pairs = [(i, i + by) for i in range(peers) if 0 <= i + by < peers]
    return lax.ppermute(x, axis, pairs)


def section_layer(window_ids, hidden, gain_row, proj_qkv, proj_out):
    row_count = hidden.shape[0]
    width_heads = proj_out.shape[0]
    head_count = width_heads // HEAD
    widened = hidden.astype(jnp.float32)
    spread = lax.rsqrt(jnp.mean(widened * widened, axis=-1, keepdims=True) + 1e-06)
    normed = (widened * spread * gain_row).astype(jnp.bfloat16)
    packed = jnp.dot(normed, proj_qkv, preferred_element_type=jnp.float32).astype(jnp.bfloat16)
    queries = packed[:, :width_heads].reshape(row_count, head_count, HEAD)
    key_rows = packed[:, width_heads : 2 * width_heads].reshape(row_count, head_count, HEAD)
    values = packed[:, 2 * width_heads :].reshape(row_count, head_count, HEAD)
    scores = jnp.einsum(
        "qhd,khd->hqk", queries, key_rows, preferred_element_type=jnp.float32
    ) * HEAD ** (-0.5)
    same_window = window_ids[:, None] == window_ids[None, :]
    scores = jnp.where(same_window[None], scores, -1e30)
    weights = jax.nn.softmax(scores, axis=-1).astype(jnp.bfloat16)
    attended = jnp.einsum("hqk,khd->qhd", weights, values, preferred_element_type=jnp.float32)
    attended = attended.astype(jnp.bfloat16).reshape(row_count, width_heads)
    mixture = jnp.dot(attended, proj_out, preferred_element_type=jnp.float32)
    return (widened + mixture).astype(jnp.bfloat16)


def on_device(patches, windows, gain, w_qkv, w_out, cotangent):
    sections = lax.axis_size("section")
    section_now = lax.axis_index("section")
    micro_count = patches.shape[0]
    gain_row = gain[0]
    proj_qkv = w_qkv[0]
    proj_out = w_out[0]
    tick_count = micro_count + sections - 1
    slot_ids = jnp.arange(micro_count)
    stored_inputs = jnp.zeros_like(patches)
    layer_outputs = jnp.zeros_like(patches)
    outgoing = jnp.zeros(patches.shape[1:], jnp.bfloat16)
    for instant in range(tick_count):
        if instant > 0:
            arrived = from_behind(outgoing, "section", 1)
        else:
            arrived = outgoing
        micro_index = instant - section_now
        active = (micro_index >= 0) & (micro_index < micro_count)
        chosen = jnp.clip(micro_index, 0, micro_count - 1)
        entering = lax.dynamic_index_in_dim(patches, chosen, 0, keepdims=False)
        window_ids = lax.dynamic_index_in_dim(windows, chosen, 0, keepdims=False)
        hidden = jnp.where(section_now == 0, entering, arrived)

        def run_forward():
            return section_layer(window_ids, hidden, gain_row, proj_qkv, proj_out)

        def keep_input():
            return hidden

        result = lax.cond(active, run_forward, keep_input)
        landing = (slot_ids == micro_index)[:, None, None]
        stored_inputs = jnp.where(landing, hidden[None], stored_inputs)
        layer_outputs = jnp.where(landing, result[None], layer_outputs)
        outgoing = result
    carry_type = jnp.bfloat16
    sum_qkv = jnp.zeros(proj_qkv.shape, carry_type)
    sum_out = jnp.zeros(proj_out.shape, carry_type)
    sum_gain = jnp.zeros(gain_row.shape, jnp.float32)
    back_grads = jnp.zeros_like(patches)
    returning = jnp.zeros(patches.shape[1:], jnp.bfloat16)
    for instant in range(tick_count):
        if instant > 0:
            arrived = from_behind(returning, "section", -1)
        else:
            arrived = returning
        micro_index = instant - (sections - 1 - section_now)
        active = (micro_index >= 0) & (micro_index < micro_count)
        chosen = jnp.clip(micro_index, 0, micro_count - 1)
        upstream = lax.dynamic_index_in_dim(cotangent, chosen, 0, keepdims=False)
        window_ids = lax.dynamic_index_in_dim(windows, chosen, 0, keepdims=False)
        hidden = lax.dynamic_index_in_dim(stored_inputs, chosen, 0, keepdims=False)
        incoming = jnp.where(section_now == sections - 1, upstream, arrived)

        def run_backward():

            def local_layer(state_in, gain_in, qkv_in, out_in):
                return section_layer(window_ids, state_in, gain_in, qkv_in, out_in)

            unused, puller = jax.vjp(local_layer, hidden, gain_row, proj_qkv, proj_out)
            d_hidden, d_gain, d_qkv, d_out = puller(incoming)
            return (d_hidden, d_gain, d_qkv, d_out)

        def skip_backward():
            return (
                jnp.zeros_like(hidden),
                jnp.zeros(gain_row.shape, jnp.float32),
                jnp.zeros(proj_qkv.shape, jnp.bfloat16),
                jnp.zeros(proj_out.shape, jnp.bfloat16),
            )

        d_hidden, d_gain, d_qkv, d_out = lax.cond(active, run_backward, skip_backward)
        sum_qkv = sum_qkv + d_qkv
        sum_out = sum_out + d_out
        sum_gain = sum_gain + d_gain
        landing = (slot_ids == micro_index)[:, None, None]
        back_grads = jnp.where(landing, d_hidden[None], back_grads)
        returning = d_hidden
    final_qkv, final_out, final_gain = (
        lax.psum_scatter(
            sum_qkv.astype(jnp.float32), ("dp", "mp"), scatter_dimension=0, tiled=True
        ),
        lax.psum_scatter(
            sum_out.astype(jnp.float32), ("dp", "mp"), scatter_dimension=1, tiled=True
        ),
        lax.psum_scatter(sum_gain, ("dp", "mp"), scatter_dimension=0, tiled=True),
    )
    return (
        layer_outputs[None],
        back_grads[None],
        final_qkv[None],
        final_out[None],
        final_gain[None],
    )


def solution(mesh):
    in_specs = (
        P(None, ("dp", "mp"), None),
        P(None, ("dp", "mp")),
        P("section", None),
        P("section", None, None),
        P("section", None, None),
        P(None, ("dp", "mp"), None),
    )
    out_specs = (
        P("section", None, ("dp", "mp"), None),
        P("section", None, ("dp", "mp"), None),
        P("section", ("dp", "mp"), None),
        P("section", None, ("dp", "mp")),
        P("section", ("dp", "mp")),
    )
    return jax.shard_map(
        on_device, mesh=mesh, in_specs=in_specs, out_specs=out_specs, check_vma=False
    )
```

profile of v0, /device:TPU:1, one launch (start us, length us, event | category | flops | bytes accessed | tf_op | source)
XLA Modules:
  0.0 493.3 jit_solution(244764036869312957)
XLA Ops:
  7.2 1.0 bitcast_select_fusion.3
  8.2 7.2 %conditional.8 = (bf16[128,1280]{1,0:T(8,128)(2,1)S(1)}) conditional(s32[]{:T(128)} %convert_element_type.377, bf16[128,1280]{1,0:T(8,128)(2,1)S(1)} %bitcast_select_fusion.3, (bf16[128,1280]{1,0:T(8,128)(2,1)S(1)}, f32[1,1280]{1,0:T(1,128)}, bf16[1280,1920]{1,0:T(8,128)(2,1)}, s32[128]{0:T(128)}, bf16[640,1280]{1,0:T(8,128)(2,1)}) %tuple.165), branch_computations={%region_0.1_spmd, %region_1.5_spmd} | conditional | flops 904938880 | bytes 19146280 | solution.py:68
  10.0 3.5 convolution_convert_fusion
  15.4 1.3 collective-permute-start
  16.8 4.0 collective-permute-done
  20.9 14.4 %collective-permute-start.1 = (bf16[128,1280]{1,0:T(8,128)(2,1)S(1)}, bf16[128,1280]{1,0:T(8,128)(2,1)S(1)}, u32[]{:S(2)}, u32[]{:S(2)}) collective-permute-start(bf16[128,1280]{1,0:T(8,128)(2,1)S(1)} %get-tuple-element.319), channel_id=1, source_target_pairs={{0,8},{8,16},{16,24},{1,9},{9,17},{17,25},{2,10},{10,18},{18,26},{... | collective-permute-start | bytes 983048 | tf_op jit(solution)/shard_map/ppermute | solution.py:12
  35.3 4.0 collective-permute-done.1
  39.4 4.0 collective-permute-start.2
  43.4 3.9 collective-permute-done.2
  47.3 1.0 select_select_fusion
  48.4 3.2 conditional.12
  48.6 2.5 broadcast.472
  51.6 1.3 collective-permute-start.3
  52.9 16.4 %collective-permute-done.3 = bf16[128,1280]{1,0:T(8,128)(2,1)} collective-permute-done((bf16[128,1280]{1,0:T(8,128)(2,1)S(1)}, bf16[128,1280]{1,0:T(8,128)(2,1)}, u32[]{:S(2)}, u32[]{:S(2)}) %collective-permute-start.3) | collective-permute-done | bytes 327712 | tf_op jit(solution)/shard_map/ppermute | solution.py:12
  69.4 4.7 conditional.13
  70.1 1.3 broadcast.488.clone
  71.4 2.5 broadcast.487
  74.1 1.3 collective-permute-start.4
  75.4 7.2 %collective-permute-done.4 = bf16[128,1280]{1,0:T(8,128)(2,1)S(1)} collective-permute-done((bf16[128,1280]{1,0:T(8,128)(2,1)}, bf16[128,1280]{1,0:T(8,128)(2,1)S(1)}, u32[]{:S(2)}, u32[]{:S(2)}) %collective-permute-start.4) | collective-permute-done | bytes 327712 | tf_op jit(solution)/shard_map/ppermute | solution.py:12
  82.6 4.1 conditional.14
  82.6 1.3 broadcast.503.clone
  83.9 2.6 broadcast.502
  86.7 1.3 collective-permute-start.5
  88.0 109.6 %collective-permute-done.5 = bf16[128,1280]{1,0:T(8,128)(2,1)} collective-permute-done((bf16[128,1280]{1,0:T(8,128)(2,1)S(1)}, bf16[128,1280]{1,0:T(8,128)(2,1)}, u32[]{:S(2)}, u32[]{:S(2)}) %collective-permute-start.5) | collective-permute-done | bytes 327712 | tf_op jit(solution)/shard_map/ppermute | solution.py:12
  197.6 38.2 %conditional.15 = (bf16[128,1280]{1,0:T(8,128)(2,1)S(1)}, f32[1280]{0:T(1024)S(1)}, bf16[1280,1920]{1,0:T(8,128)(2,1)S(1)}, bf16[640,1280]{0,1:T(8,128)(2,1)S(1)}) conditional(s32[]{:T(128)} %convert_element_type.378, () %tuple.73, (pred[]{:T(512)}, bf16[128,1280]{1,0:T(8,128)(2,1)S(1)}, bf16[128,1280]{1,0:T(8,128)(2,1)}, ...), branch_computations={%region_44.45_spmd, %region_45.52_spmd} | conditional | flops 2532988928 | bytes 46233264 | solution.py:109
  197.8 1.0 broadcast_select_fusion.3
  200.6 2.1 convolution_convert_fusion.47
  202.8 3.4 convolution_convert_fusion.41
  207.7 1.1 copy.171
  209.6 2.2 fusion.155
  211.7 2.1 multiply_reduce_fusion.3
  213.9 1.5 convolution_convert_fusion.43
  215.4 2.3 convolution_convert_fusion.46
  217.7 2.5 convolution_convert_fusion.44
  220.2 2.4 convolution_convert_fusion.45
  222.6 4.2 fusion.128
  226.8 1.0 fusion.129
  227.8 1.8 convolution_convert_fusion.39
  229.6 3.5 copy.208
  233.1 2.6 convolution_convert_fusion.38
  235.8 5.8 %add_convert_fusion.1 = f32[640,1280]{0,1:T(8,128)} fusion(bf16[640,1280]{0,1:T(8,128)(2,1)S(1)} %get-tuple-element.225, bf16[640,1280]{0,1:T(8,128)(2,1)} %get-tuple-element.224, bf16[640,1280]{0,1:T(8,128)(2,1)S(1)} %get-tuple-element.222, bf16[640,1280]{0,1:T(8,128)(2,1)} %get-tuple-element.223), kind=kLoop, calls=%fused_computation.265 | loop fusion | flops 3276800 | bytes 9830400 | tf_op jit(solution)/shard_map/convert_element_type | solution.py:121
  241.6 11.5 %add_convert_fusion = f32[1280,1920]{1,0:T(8,128)} fusion(bf16[1280,1920]{1,0:T(8,128)(2,1)} %copy-done.4, bf16[1280,1920]{1,0:T(8,128)(2,1)} %get-tuple-element.207, bf16[1280,1920]{1,0:T(8,128)(2,1)} %get-tuple-element.205, bf16[1280,1920]{1,0:T(8,128)(2,1)} %get-tuple-element.206), kind=kLoop, calls=%fused_computation.264 | loop fusion | flops 9830400 | bytes 29491200 | tf_op jit(solution)/shard_map/convert_element_type | solution.py:118
  255.5 143.4 %all-reduce.14 = f32[1280]{0:T(1024)S(1)} all-reduce(f32[1280]{0:T(1024)S(1)} %add_add_fusion.4), channel_id=4, replica_groups=mesh['dp'=8,'section'=4,'mp'=8] {'dp','mp'}, use_global_device_ids=true, to_apply=%region_54.55.clone | all-reduce | flops 1280 | bytes 10240
  399.4 1.9 select_bitcast_fusion
  401.4 81.2 %all-reduce.18.cloned.1.call-done = (f32[1280,1920]{1,0:T(8,128)}, f32[640,1280]{0,1:T(8,128)}) async-done(((f32[1280,1920]{1,0:T(8,128)}, f32[640,1280]{0,1:T(8,128)}), (f32[1280,1920]{1,0:T(8,128)}, f32[640,1280]{0,1:T(8,128)})) %all-reduce.18.cloned.1.call-update) | async-done | bytes 13107216
  482.5 1.0 dynamic-slice_bitcast_fusion
  483.5 0.9 dynamic-slice_bitcast_fusion.1
  484.4 0.8 copy.179
  (82 shorter events, 11.9 us)
Async XLA Ops:
  7.2 475.4 %all-reduce.18.cloned.1.call-start = ((), (), s32[]{:S(2)}) async-start(), calls=%async_computation | async-start | bytes 26214400
  8.2 12.5 %copy-start.7 = (bf16[1,128,1280]{2,1,0:T(8,128)(2,1)S(1)}, bf16[1,128,1280]{2,1,0:T(8,128)(2,1)}, u32[]{:S(2)}) copy-start(bf16[1,128,1280]{2,1,0:T(8,128)(2,1)} %param.22) | copy-start | bytes 983044
  10.0 5.0 %copy-start.1 = (bf16[640,1280]{1,0:T(8,128)(2,1)S(1)}, bf16[640,1280]{1,0:T(8,128)(2,1)}, u32[]{:S(2)}) copy-start(bf16[640,1280]{1,0:T(8,128)(2,1)} %get-tuple-element.132) | copy-start | bytes 4915204 | tf_op jit(solution)/shard_map/cond
  15.4 5.3 %collective-permute-start = (bf16[128,1280]{1,0:T(8,128)(2,1)S(1)}, bf16[128,1280]{1,0:T(8,128)(2,1)S(1)}, u32[]{:S(2)}, u32[]{:S(2)}) collective-permute-start(bf16[128,1280]{1,0:T(8,128)(2,1)S(1)} %get-tuple-element.318), channel_id=1, source_target_pairs={{0,8},{8,16},{16,24},{1,9},{9,17},{17,25},{2,10},{10,18},{18,26},{... | collective-permute-start | bytes 983048 | tf_op jit(solution)/shard_map/ppermute | solution.py:12
  20.8 14.4 %copy-start.14 = (bf16[128,1280]{1,0:T(8,128)(2,1)}, bf16[128,1280]{1,0:T(8,128)(2,1)S(1)}, u32[]{:S(2)}) copy-start(bf16[128,1280]{1,0:T(8,128)(2,1)S(1)} %get-tuple-element.319) | copy-start | bytes 983044
  20.9 18.4 %collective-permute-start.1 = (bf16[128,1280]{1,0:T(8,128)(2,1)S(1)}, bf16[128,1280]{1,0:T(8,128)(2,1)S(1)}, u32[]{:S(2)}, u32[]{:S(2)}) collective-permute-start(bf16[128,1280]{1,0:T(8,128)(2,1)S(1)} %get-tuple-element.319), channel_id=1, source_target_pairs={{0,8},{8,16},{16,24},{1,9},{9,17},{17,25},{2,10},{10,18},{18,26},{... | collective-permute-start | bytes 983048 | tf_op jit(solution)/shard_map/ppermute | solution.py:12
  39.3 9.1 %copy-start.6 = (bf16[1,128,1280]{2,1,0:T(8,128)(2,1)S(1)}, bf16[1,128,1280]{2,1,0:T(8,128)(2,1)}, u32[]{:S(2)}) copy-start(bf16[1,128,1280]{2,1,0:T(8,128)(2,1)} %param.27) | copy-start | bytes 983044
  39.3 4.0 copy-start.15
  39.4 8.0 %collective-permute-start.2 = (bf16[128,1280]{1,0:T(8,128)(2,1)S(1)}, bf16[128,1280]{1,0:T(8,128)(2,1)S(1)}, u32[]{:S(2)}, u32[]{:S(2)}) collective-permute-start(bf16[128,1280]{1,0:T(8,128)(2,1)S(1)} %get-tuple-element.320), channel_id=1, source_target_pairs={{0,8},{8,16},{16,24},{1,9},{9,17},{17,25},{2,10},{10,18},{18,26},{... | collective-permute-start | bytes 983048 | tf_op jit(solution)/shard_map/ppermute | solution.py:12
  51.6 17.8 %copy-start.8 = (bf16[128,1280]{1,0:T(8,128)(2,1)}, bf16[128,1280]{1,0:T(8,128)(2,1)S(1)}, u32[]{:S(2)}) copy-start(bf16[128,1280]{1,0:T(8,128)(2,1)S(1)} %get-tuple-element.201) | copy-start | bytes 983044
  51.6 17.7 %collective-permute-start.3 = (bf16[128,1280]{1,0:T(8,128)(2,1)S(1)}, bf16[128,1280]{1,0:T(8,128)(2,1)}, u32[]{:S(2)}, u32[]{:S(2)}) collective-permute-start(bf16[128,1280]{1,0:T(8,128)(2,1)S(1)} %get-tuple-element.201), channel_id=1, source_target_pairs={{8,0},{16,8},{24,16},{9,1},{17,9},{25,17},{10,2},{18,10},{26,18},{... | collective-permute-start | bytes 983048 | tf_op jit(solution)/shard_map/ppermute | solution.py:12
  74.1 8.5 %collective-permute-start.4 = (bf16[128,1280]{1,0:T(8,128)(2,1)}, bf16[128,1280]{1,0:T(8,128)(2,1)S(1)}, u32[]{:S(2)}, u32[]{:S(2)}) collective-permute-start(bf16[128,1280]{1,0:T(8,128)(2,1)} %get-tuple-element.202), channel_id=1, source_target_pairs={{8,0},{16,8},{24,16},{9,1},{17,9},{25,17},{10,2},{18,10},{26,18},{... | collective-permute-start | bytes 983048 | tf_op jit(solution)/shard_map/ppermute | solution.py:12
  86.7 110.9 %copy-start.11 = (bf16[128,1280]{1,0:T(8,128)(2,1)}, bf16[128,1280]{1,0:T(8,128)(2,1)S(1)}, u32[]{:S(2)}) copy-start(bf16[128,1280]{1,0:T(8,128)(2,1)S(1)} %get-tuple-element.203) | copy-start | bytes 983044
  86.7 110.9 %collective-permute-start.5 = (bf16[128,1280]{1,0:T(8,128)(2,1)S(1)}, bf16[128,1280]{1,0:T(8,128)(2,1)}, u32[]{:S(2)}, u32[]{:S(2)}) collective-permute-start(bf16[128,1280]{1,0:T(8,128)(2,1)S(1)} %get-tuple-element.203), channel_id=1, source_target_pairs={{8,0},{16,8},{24,16},{9,1},{17,9},{25,17},{10,2},{18,10},{26,18},{... | collective-permute-start | bytes 983048 | tf_op jit(solution)/shard_map/ppermute | solution.py:12
  215.4 4.8 copy-start.22
  217.7 4.9 copy-start.26
  226.7 6.4 %copy-start.28 = (bf16[8,128,80]{1,2,0:T(8,128)(2,1)S(1)}, bf16[8,128,80]{1,2,0:T(8,128)(2,1)}, u32[]{:S(2)}) copy-start(bf16[8,128,80]{1,2,0:T(8,128)(2,1)} %convolution_convert_fusion.44) | copy-start | bytes 491524 | tf_op jit(solution)/shard_map/cond
  233.1 2.7 copy-start.5
  233.1 2.7 copy-start.12
  235.8 5.9 %copy-start.4 = (bf16[1280,1920]{1,0:T(8,128)(2,1)}, bf16[1280,1920]{1,0:T(8,128)(2,1)S(1)}, u32[]{:S(2)}) copy-start(bf16[1280,1920]{1,0:T(8,128)(2,1)S(1)} %get-tuple-element.208) | copy-start | bytes 14745604
  235.8 5.9 %copy-start.13 = (bf16[128,1280]{1,0:T(8,128)(2,1)}, bf16[128,1280]{1,0:T(8,128)(2,1)S(1)}, u32[]{:S(2)}) copy-start(bf16[128,1280]{1,0:T(8,128)(2,1)S(1)} %get-tuple-element.204) | copy-start | bytes 983044
  253.2 0.7 copy-start.30
  253.2 1.9 copy-start
  253.2 1.9 copy-start.19
  253.2 1.9 copy-start.29
  255.1 144.3 %copy-start.9 = (bf16[128,1280]{1,0:T(8,128)(2,1)S(1)}, bf16[128,1280]{1,0:T(8,128)(2,1)}, u32[]{:S(2)}) copy-start(bf16[128,1280]{1,0:T(8,128)(2,1)} %copy-done.8) | copy-start | bytes 983044
Sparse Core Ops, SparseCore 0:
  253.3 229.1 all-reduce.17
where the time goes:
time: 502 us; the launch traced here: 493 us
  waiting for transfers between devices  226 us (45%)
  blocking collectives  143 us (28%)
  matrix products  31.8 us (6%)
  other arithmetic  26.8 us (5%)
  local copies, waits for them, and re-layouts  24.1 us (5%)
  starting transfers between devices  23.6 us (5%)
  between operations  15.6 us (3%)
    ppermute x6, waiting for transfers between devices, from_behind(): return lax.ppermute(x, axis, pairs)  145 us
    unnamed x1, blocking collectives  143 us
    unnamed x2, waiting for transfers between devices  81.2 us
    ppermute x6, starting transfers between devices, from_behind(): return lax.ppermute(x, axis, pairs)  23.6 us
    dot_general x4, matrix products, section_layer(): jnp.dot(normed, proj_qkv, preferred_element_type=jnp.float32)  13.6 us
    convert_element_type x1, other arithmetic, on_device(): sum_qkv.astype(jnp.float32)  11.5 us
    another operation x13, local copies, waits for them, and re-layouts  11.2 us
  transfers between devices with their start and end apart: 7, of which 7 were waited for; matrix products, arithmetic and copies ran while one was open for 1% of the time, Pallas kernels for 0%

commit v1 on v0

v1 whole, which is shorter than its diff:
```python
import jax
import jax.numpy as jnp
from jax import lax
from jax.experimental import pallas as pl
from jax.experimental.pallas import tpu as pltpu
from jax.sharding import PartitionSpec as P

HEAD = 80
HEADS = 8
ROWS = 128
VD = 1280
HW = 640
NM = 8
NZ = 8
NS = 4
CHUNKS = 2
CR = ROWS // CHUNKS
ZR = VD // NZ
FR = ZR // NM
SCALE = HEAD**-0.5
MESH = pl.DeviceIdType.MESH
F32 = jnp.float32
BF16 = jnp.bfloat16


def nt(a, b):
    return lax.dot_general(a, b, (((1,), (1,)), ((), ())), preferred_element_type=F32)


def nn(a, b):
    return lax.dot_general(a, b, (((1,), (0,)), ((), ())), preferred_element_type=F32)


def tn(a, b):
    return lax.dot_general(a, b, (((0,), (0,)), ((), ())), preferred_element_type=F32)


def head_span(h):
    lo = HEAD * h
    t0 = lo // 128 * 128
    t1 = -(-(lo + HEAD) // 128) * 128
    return lo, t0, t1


def masked(x, h):
    lo, t0, t1 = head_span(h)
    cols = lax.broadcasted_iota(jnp.int32, (ROWS, t1 - t0), 1) + t0
    return jnp.where((cols >= lo) & (cols < lo + HEAD), x, jnp.zeros_like(x))


def add_head(acc, h, value):
    lo, t0, t1 = head_span(h)
    for t in range(t0, t1, 128):
        part = value[:, t - t0 : t - t0 + 128]
        if h > 0 and t < -(-lo // 128) * 128 and lo % 128 != 0 and t <= lo:
            acc[:, t : t + 128] += part
        else:
            acc[:, t : t + 128] = part


def kernel(
    patches, cot, win_row, win_col, gain, wq_hbm, wo_hbm,
    act, gin, out_q, out_o, out_gain,
    wq, wo, hbuf, gbuf, normed, packed, pt32, ptb, att, acc, acc2, datt, dp,
    ngt, atg, dpt, gt32, gperm, dpg, gpg, dgain, dgrecv, dgz, dgzrecv,
    rq, ro, sq, so, zq, zo, fin, finrecv, total,
    w_sem, hs, hr, gs, gr, ns, nr, as_, ar, ds, dr, ps, pr, vs, vr, us, ur, qs, qr, os_, or_, fs, fr,
):
    s = lax.axis_index("section")
    m = lax.axis_index("mp")
    z = lax.axis_index("dp")
    copies = []
    for i in range(3):
        cols = pl.ds(i * HW, HW)
        copies.append(pltpu.make_async_copy(wq_hbm.at[:, cols], wq.at[:, cols], w_sem.at[i]))
    copies.append(pltpu.make_async_copy(wo_hbm, wo, w_sem.at[3]))
    for c in copies:
        c.start()

    barrier = pltpu.get_barrier_semaphore()
    for d in range(1, NM):
        pl.semaphore_signal(barrier, inc=1, device_id={"mp": lax.rem(m + d, NM)}, device_id_type=MESH)
    for d in range(1, NZ):
        pl.semaphore_signal(barrier, inc=1, device_id={"dp": lax.rem(z + d, NZ)}, device_id_type=MESH)
    for d in (1, NS - 1):
        pl.semaphore_signal(barrier, inc=1, device_id={"section": lax.rem(s + d, NS)}, device_id_type=MESH)

    def remote(src, dst, ssem, rsem, where):
        return pltpu.make_async_remote_copy(
            src_ref=src, dst_ref=dst, send_sem=ssem, recv_sem=rsem, device_id=where, device_id_type=MESH
        )

    def rows_of(c):
        return pl.ds(c * CR, CR)

    def hop_forward(c):
        return remote(
            act.at[rows_of(c)], hbuf.at[rows_of(c)], hs.at[c], hr.at[c], {"section": lax.rem(s + 1, NS)}
        )

    def hop_back(c):
        return remote(
            gin.at[rows_of(c)], gbuf.at[rows_of(c)], gs.at[c], gr.at[c], {"section": lax.rem(s + NS - 1, NS)}
        )

    def mp_lanes(i):
        return pl.ds(pl.multiple_of(i * ROWS, ROWS), ROWS)

    same = win_col[...] == win_row[...]

    @pl.when(s == 0)
    def _():
        hbuf[...] = patches[...]

    pl.semaphore_wait(barrier, (NM - 1) + (NZ - 1) + 2)

    for c in range(CHUNKS):
        rows = rows_of(c)

        @pl.when(s > 0)
        def _():
            hop_forward(c).wait_recv()

        wide = hbuf[rows, :].astype(F32)
        spread = lax.rsqrt(jnp.mean(wide * wide, axis=-1, keepdims=True) + 1e-6)
        normed[rows, :] = (wide * spread * gain[...]).astype(BF16)
        for i in range(3):
            if c == 0:
                copies[i].wait()
            packed[rows, i * HW : (i + 1) * HW] = nn(
                normed[rows, :], wq[:, i * HW : (i + 1) * HW]
            ).astype(BF16)
    copies[3].wait()

    for h in range(HEADS):
        lo, t0, t1 = head_span(h)
        q = packed[:, t0:t1]
        k = masked(packed[:, HW + t0 : HW + t1], h)
        scores = nt(k, q) * SCALE
        scores = jnp.where(same, scores, -1e30)
        top = jnp.max(scores, axis=0, keepdims=True)
        e = jnp.exp(scores - top)
        p = e / jnp.sum(e, axis=0, keepdims=True)
        pt32[h] = p
        ptb[h] = p.astype(BF16)
    for h in range(HEADS):
        lo, t0, t1 = head_span(h)
        v = masked(packed[:, 2 * HW + t0 : 2 * HW + t1], h)
        add_head(acc, h, tn(ptb[h], v))
    att[...] = acc[...].astype(BF16)

    def project(c):
        rows = rows_of(c)
        act[rows, :] = (hbuf[rows, :].astype(F32) + nn(att[rows, :], wo[...])).astype(BF16)

    chip = m // 2
    core = lax.rem(m, 2)
    sibling = chip * 2 + 1 - core

    def gather_copies(slot, i, to):
        lanes = mp_lanes(slot)
        return (
            remote(ngt.at[:, lanes], ngt.at[:, lanes], ns.at[i], nr.at[i], {"mp": to}),
            remote(atg.at[lanes, :], atg.at[lanes, :], as_.at[i], ar.at[i], {"mp": to}),
        )

    def across(d):
        return lax.rem(chip + d, NM // 2) * 2 + core

    def gather_start():
        ngt[:, mp_lanes(m)] = normed[...].T
        atg[mp_lanes(m), :] = att[...]
        for d in range(1, NM // 2):
            for c in gather_copies(m, d, across(d)):
                c.start()
        for c in gather_copies(m, 0, sibling):
            c.start()

    def gather_forward():
        for d in range(1, NM // 2):
            source = across(NM // 2 - d)
            for c in gather_copies(source, d, across(d)):
                c.wait_recv()
            for c in gather_copies(source, NM // 2 - 1 + d, sibling):
                c.start()

    def gather_finish():
        for c in gather_copies(sibling, 0, sibling):
            c.wait_recv()
        for d in range(1, NM // 2):
            source = lax.rem(chip + NM // 2 - d, NM // 2) * 2 + 1 - core
            for c in gather_copies(source, NM // 2 - 1 + d, sibling):
                c.wait_recv()

    def gather_drain():
        for i in range(NM - 1):
            for c in gather_copies(m, i, sibling):
                c.wait_send()

    @pl.when(s < NS - 1)
    def _():
        for c in range(CHUNKS):
            project(c)
            hop_forward(c).start()
        gather_start()
        gather_forward()

    @pl.when(s == NS - 1)
    def _():
        gbuf[...] = cot[...]

    for c in range(CHUNKS):
        rows = rows_of(c)

        @pl.when(s < NS - 1)
        def _():
            hop_back(c).wait_recv()

        datt[rows, :] = nt(gbuf[rows, :], wo[...]).astype(BF16)

    for h in range(HEADS):
        lo, t0, t1 = head_span(h)
        q = masked(packed[:, t0:t1], h)
        k = masked(packed[:, HW + t0 : HW + t1], h)
        v = masked(packed[:, 2 * HW + t0 : 2 * HW + t1], h)
        da = datt[:, t0:t1]
        dprob = nt(v, da).astype(BF16).astype(F32)
        p = pt32[h]
        dsc = p * (dprob - jnp.sum(p * dprob, axis=0, keepdims=True))
        dsc = (dsc * SCALE).astype(BF16)
        add_head(acc, h, tn(dsc, k))
        add_head(acc2, h, nn(dsc, q))
        add_head(total, h, nn(ptb[h], masked(da, h)))
    dp[:, 0:HW] = acc[...].astype(BF16)
    dp[:, HW : 2 * HW] = acc2[...].astype(BF16)
    dp[:, 2 * HW : 3 * HW] = total[...].astype(BF16)

    def column_copies(d):
        to = lax.rem(m + d, NM)
        rows = pl.ds(pl.multiple_of(to * 256, 256), 256)
        lanes = mp_lanes(m)
        return (
            remote(dpt.at[rows], dpg.at[:, lanes], ds.at[d], dr.at[d], {"mp": to}),
            remote(gperm.at[rows], gpg.at[:, lanes], ps.at[d], pr.at[d], {"mp": to}),
        )

    def columns_q():
        dpt[0 : 3 * HW, :] = dp[...].T
        dpt[3 * HW : 2048, :] = jnp.zeros((128, ROWS), BF16)
        for d in range(1, NM):
            column_copies(d)[0].start()
        dpg[:, mp_lanes(m)] = dpt[pl.ds(pl.multiple_of(m * 256, 256), 256), :]

    def columns_g():
        gt32[0:VD, :] = gbuf[...].astype(F32).T
        gt32[VD : VD + 32, :] = jnp.zeros((32, ROWS), F32)
        for i in range(NM):
            for j in range(NZ):
                first = FR * (NM * j + i)
                gperm[i * 256 + j * 32 : i * 256 + j * 32 + 32, :] = gt32[first : first + 32, :].astype(BF16)
        for d in range(1, NM):
            column_copies(d)[1].start()
        gpg[:, mp_lanes(m)] = gperm[pl.ds(pl.multiple_of(m * 256, 256), 256), :]

    @pl.when(s == 0)
    def _():
        columns_q()

    for c in range(CHUNKS):
        rows = rows_of(c)
        dn = nt(dp[rows, :], wq[...]).astype(BF16).astype(F32)
        wide = hbuf[rows, :].astype(F32)
        spread = lax.rsqrt(jnp.mean(wide * wide, axis=-1, keepdims=True) + 1e-6)
        lifted = dn * gain[...]
        inner = jnp.mean(lifted * wide, axis=-1, keepdims=True)
        back = gbuf[rows, :].astype(F32) + spread * lifted - wide * (spread * spread * spread * inner)
        gin[rows, :] = back.astype(BF16)

        @pl.when(s > 0)
        def _():
            hop_back(c).start()

        part = jnp.sum(dn * (wide * spread), axis=0, keepdims=True)
        if c == 0:
            dgain[0] = part
        else:
            dgain[0] += part

    @pl.when(s > 0)
    def _():
        columns_q()

    @pl.when(s == NS - 1)
    def _():
        for c in range(CHUNKS):
            project(c)
        gather_start()
        gather_forward()

    columns_g()

    def gain_mp(d):
        return remote(dgain.at[0], dgrecv.at[d], vs.at[d], vr.at[d], {"mp": lax.rem(m + d, NM)})

    def gain_dp(d):
        return remote(dgz.at[0], dgzrecv.at[d], us.at[d], ur.at[d], {"dp": lax.rem(z + d, NZ)})

    for d in range(1, NM):
        gain_mp(d).start()

    gather_finish()
    for d in range(1, NM):
        column_copies(d)[0].wait_recv()

    def chunk_q(k):
        rows = pl.ds(pl.multiple_of(k * ZR, 16), ZR)
        return nt(ngt[rows, :], dpg[...])

    def chunk_o(k):
        rows = pl.ds(pl.multiple_of(k * 32, 32), 32)
        return nn(gpg[rows, :], atg[...])

    up = {"dp": lax.rem(z + 1, NZ)}
    down = {"dp": lax.rem(z + NZ - 1, NZ)}

    def ring_q(t):
        return remote(sq.at[t], zq.at[t], qs.at[t], qr.at[t], up if t < 4 else down)

    def ring_o(t):
        return remote(so.at[t], zo.at[t], os_.at[t], or_.at[t], up if t < 4 else down)

    def owner(t):
        if t < 4:
            return lax.rem(z + 4 - t, NZ)
        return lax.rem(z + NZ - 3 + (t - 4), NZ)

    for t in (0, 4):
        sq[t] = chunk_q(owner(t)).astype(BF16)
        ring_q(t).start()
    for d in range(1, NM):
        column_copies(d)[1].wait_recv()
    for t in (0, 4):
        so[t] = chunk_o(owner(t)).astype(BF16)
        ring_o(t).start()
    sum_gain = dgain[0]
    for d in range(1, NM):
        gain_mp(d).wait_recv()
        sum_gain = sum_gain + dgrecv[d]
    dgz[0] = sum_gain
    for d in range(1, NZ):
        gain_dp(d).start()
    for t in (1, 5, 2, 6, 3):
        mine = chunk_q(owner(t))
        ring_q(t - 1).wait_recv()
        sq[t] = (mine + zq[t - 1].astype(F32)).astype(BF16)
        ring_q(t).start()
        mine = chunk_o(owner(t))
        ring_o(t - 1).wait_recv()
        so[t] = (mine + zo[t - 1].astype(F32)).astype(BF16)
        ring_o(t).start()
    rq[0:ZR, :] = chunk_q(z)
    ro[...] = chunk_o(z)
    for t in (6, 3):
        ring_q(t).wait_recv()
        rq[0:ZR, :] += zq[t].astype(F32)

    def piece(d):
        return remote(fin.at[lax.rem(m + d, NM)], finrecv.at[m], fs.at[d], fr.at[d], {"mp": lax.rem(m + d, NM)})

    for i in range(NM):
        if FR * i + 24 <= ZR:
            fin[i] = rq[FR * i : FR * i + 24, :]
        else:
            fin[i, 0:FR] = rq[FR * i : FR * i + FR, :]
            fin[i, FR:24] = jnp.zeros((24 - FR, 256), F32)
    for d in range(1, NM):
        piece(d).start()
    finrecv[m] = fin[m]

    for t in (6, 3):
        ring_o(t).wait_recv()
        ro[...] += zo[t].astype(F32)
    out_o[...] = ro[...].T[:, 0:FR]
    sum_gain = dgz[0]
    for d in range(1, NZ):
        gain_dp(d).wait_recv()
        sum_gain = sum_gain + dgzrecv[d]
    out_gain[...] = sum_gain

    for d in range(1, NM):
        source = lax.rem(m + NM - d, NM)
        remote(fin.at[source], finrecv.at[source], fs.at[d], fr.at[d], {"mp": source}).wait_recv()
    for i in range(NM):
        wide = min(256, 3 * HW - 256 * i)
        out_q[:, 256 * i : 256 * i + wide] = finrecv[i, 0:FR, 0:wide]

    @pl.when(s < NS - 1)
    def _():
        for c in range(CHUNKS):
            hop_forward(c).wait_send()

    @pl.when(s > 0)
    def _():
        for c in range(CHUNKS):
            hop_back(c).wait_send()

    gather_drain()
    for d in range(1, NM):
        for c in column_copies(d):
            c.wait_send()
        gain_mp(d).wait_send()
        piece(d).wait_send()
    for d in range(1, NZ):
        gain_dp(d).wait_send()
    for t in range(7):
        ring_q(t).wait_send()
        ring_o(t).wait_send()


def on_device(patches, windows, gain, w_qkv, w_out, cotangent):
    vmem = pl.BlockSpec(memory_space=pltpu.VMEM)
    hbm = pl.BlockSpec(memory_space=pl.ANY)
    dma = pltpu.SemaphoreType.DMA
    scratch = [
        pltpu.VMEM((VD, 3 * HW), BF16),
        pltpu.VMEM((HW, VD), BF16),
        pltpu.VMEM((ROWS, VD), BF16),
        pltpu.VMEM((ROWS, VD), BF16),
        pltpu.VMEM((ROWS, VD), BF16),
        pltpu.VMEM((ROWS, 3 * HW), BF16),
        pltpu.VMEM((HEADS, ROWS, ROWS), F32),
        pltpu.VMEM((HEADS, ROWS, ROWS), BF16),
        pltpu.VMEM((ROWS, HW), BF16),
        pltpu.VMEM((ROWS, HW), F32),
        pltpu.VMEM((ROWS, HW), F32),
        pltpu.VMEM((ROWS, HW), BF16),
        pltpu.VMEM((ROWS, 3 * HW), BF16),
        pltpu.VMEM((VD, NM * ROWS), BF16),
        pltpu.VMEM((NM * ROWS, HW), BF16),
        pltpu.VMEM((2048, ROWS), BF16),
        pltpu.VMEM((VD + 32, ROWS), F32),
        pltpu.VMEM((2048, ROWS), BF16),
        pltpu.VMEM((256, NM * ROWS), BF16),
        pltpu.VMEM((256, NM * ROWS), BF16),
        pltpu.VMEM((1, 1, VD), F32),
        pltpu.VMEM((NM, 1, VD), F32),
        pltpu.VMEM((1, 1, VD), F32),
        pltpu.VMEM((NZ, 1, VD), F32),
        pltpu.VMEM((ZR, 256), F32),
        pltpu.VMEM((32, HW), F32),
        pltpu.VMEM((7, ZR, 256), BF16),
        pltpu.VMEM((7, 32, HW), BF16),
        pltpu.VMEM((7, ZR, 256), BF16),
        pltpu.VMEM((7, 32, HW), BF16),
        pltpu.VMEM((NM, 24, 256), F32),
        pltpu.VMEM((NM, 24, 256), F32),
        pltpu.VMEM((ROWS, HW), F32),
        dma((4,)),
        dma((CHUNKS,)), dma((CHUNKS,)), dma((CHUNKS,)), dma((CHUNKS,)),
    ] + [dma((8,)) for _ in range(18)]
    act, gin, out_q, out_o, out_gain = pl.pallas_call(
        kernel,
        out_shape=(
            jax.ShapeDtypeStruct((ROWS, VD), BF16),
            jax.ShapeDtypeStruct((ROWS, VD), BF16),
            jax.ShapeDtypeStruct((FR, 3 * HW), F32),
            jax.ShapeDtypeStruct((HW, FR), F32),
            jax.ShapeDtypeStruct((1, VD), F32),
        ),
        in_specs=[vmem] * 5 + [hbm] * 2,
        out_specs=(vmem,) * 5,
        scratch_shapes=scratch,
        compiler_params=pltpu.CompilerParams(
            collective_id=0, has_side_effects=True, vmem_limit_bytes=48 * 1024 * 1024
        ),
    )(
        patches[0], cotangent[0], windows, windows.reshape(ROWS, 1), gain, w_qkv[0], w_out[0]
    )
    place = (lax.axis_index("dp") * NM + lax.axis_index("mp")) * FR
    own_gain = lax.dynamic_slice(out_gain, (0, place), (1, FR))
    return (act[None, None], gin[None, None], out_q[None], out_o[None], own_gain)


def solution(mesh):
    in_specs = (
        P(None, ("dp", "mp"), None),
        P(None, ("dp", "mp")),
        P("section", None),
        P("section", None, None),
        P("section", None, None),
        P(None, ("dp", "mp"), None),
    )
    out_specs = (
        P("section", None, ("dp", "mp"), None),
        P("section", None, ("dp", "mp"), None),
        P("section", ("dp", "mp"), None),
        P("section", None, ("dp", "mp")),
        P("section", ("dp", "mp")),
    )
    return jax.shard_map(
        on_device, mesh=mesh, in_specs=in_specs, out_specs=out_specs, check_vma=False
    )
```

time: 502 us -> 129 us (0.26); the launches traced: 493 us -> 129 us
  waiting for transfers between devices: 226 us -> 0 us
  blocking collectives: 143 us -> 0 us
  Pallas kernels: 0 us -> 119 us
  matrix products: 31.8 us -> 0 us
  other arithmetic: 26.8 us -> 0 us
  starting transfers between devices: 23.6 us -> 0 us
  local copies, waits for them, and re-layouts: 24.1 us -> 9.1 us
  between operations: 15.6 us -> 0.66 us
    ppermute x6 -> x0, waiting for transfers between devices: 145 us -> none  [from_behind(): return lax.ppermute(x, axis, pairs)]
    unnamed x1 -> x0, blocking collectives: 143 us -> none
    pallas_call x0 -> x1, Pallas kernels: none -> 119 us  [on_device(): pl.pallas_call(kernel, out_shape=(jax.ShapeDtypeStruct((ROWS, VD), BF16),...]
    unnamed x2 -> x0, waiting for transfers between devices: 81.2 us -> none
    dot_general x14 -> x0, matrix products: 29.3 us -> none  [the longest x4 13.6 us: section_layer(): jnp.dot(normed, proj_qkv, preferred_element_type=jnp.float32)]
    ppermute x6 -> x0, starting transfers between devices: 23.6 us -> none  [from_behind(): return lax.ppermute(x, axis, pairs)]
    convert_element_type x3 -> x0, other arithmetic: 18.4 us -> none  [the longest x1 11.5 us: on_device(): sum_qkv.astype(jnp.float32)]
    another operation x13 -> x0, local copies, waits for them, and re-layouts: 11.2 us -> none
  transfers between devices with their start and end apart: 7 -> 0, of which waited for: 7 -> 0; matrix products, arithmetic and copies ran while one was open for 1% -> 0% of each run, Pallas kernels for 0% -> 0%
where the time goes in v1:
time: 129 us
  Pallas kernels  119 us (92%)
  local copies, waits for them, and re-layouts  9.1 us (7%)
    pallas_call x1, Pallas kernels, on_device(): pl.pallas_call(kernel, out_shape=(jax.ShapeDtypeStruct((ROWS, VD), BF16),...  119 us
    unnamed x14, local copies, waits for them, and re-layouts  7.75 us

profile of v1, /device:TPU:1, one launch (start us, length us, event | category | flops | bytes accessed | tf_op | source)
XLA Modules:
  0.0 128.9 jit_solution(9345800989015897330)
XLA Ops:
  0.6 0.8 copy.11.win_col
  1.4 0.0 copy-start
  1.4 1.4 %copy-done = bf16[1,640,1280]{2,1,0:T(8,128)(2,1)S(1)} copy-done((bf16[1,640,1280]{2,1,0:T(8,128)(2,1)S(1)}, bf16[1,640,1280]{2,1,0:T(8,128)(2,1)}, u32[]{:S(2)}) %copy-start) | copy-done | bytes 1638424
  2.8 0.0 copy-start.1
  2.8 1.0 copy-done.1
  3.8 0.0 copy-start.2
  3.8 1.0 copy-done.2
  4.8 0.0 copy-start.3
  4.8 0.7 copy-done.3
  5.5 0.0 copy-start.4
  5.5 0.7 copy-done.4
  6.1 119.1 %shard_map.101 = (bf16[128,1280]{1,0:T(8,128)(2,1)S(1)}, bf16[128,1280]{1,0:T(8,128)(2,1)S(1)}, f32[20,1920]{1,0:T(8,128)S(1)}, f32[640,20]{1,0:T(8,128)S(1)}, f32[1,1280]{1,0:T(1,128)S(1)}) custom-call(bf16[128,1280]{1,0:T(8,128)(2,1)S(1)} %bitcast.10, bf16[128,1280]{1,0:T(8,128)(2,1)S(1)} %bitcast.11, s32[1,128]{1,0:T(1,128)S(1)} %copy-done.4, ...), custom_call_target="tpu_custom_call" | custom-call | tf_op jit(solution)/shard_map/pallas_call | solution.py:461
  125.2 0.6 constant_dynamic-slice_fusion
  125.8 0.8 copy.13
  126.6 0.8 copy.12
  127.4 0.7 copy.16
  128.1 0.7 copy.17
Async XLA Ops:
  1.4 1.4 %copy-start = (bf16[1,640,1280]{2,1,0:T(8,128)(2,1)S(1)}, bf16[1,640,1280]{2,1,0:T(8,128)(2,1)}, u32[]{:S(2)}) copy-start(bf16[1,640,1280]{2,1,0:T(8,128)(2,1)} %param.10) | copy-start | bytes 4915204
  2.8 1.0 copy-start.1
  3.8 1.0 copy-start.2
  4.8 0.7 copy-start.3
  5.5 0.7 copy-start.4

commit v2 on v1

v2 whole, which is shorter than its diff:
```python
import jax
import jax.numpy as jnp
from jax import lax
from jax.experimental import pallas as pl
from jax.experimental.pallas import tpu as pltpu
from jax.sharding import PartitionSpec as P

HEAD = 80
HEADS = 8
ROWS = 128
VD = 1280
HW = 640
NM = 8
NZ = 8
NS = 4
CHUNKS = 5
CW = VD // CHUNKS
ZR = VD // NZ
FR = ZR // NM
SCALE = HEAD**-0.5
MESH = pl.DeviceIdType.MESH
F32 = jnp.float32
BF16 = jnp.bfloat16


def nt(a, b):
    return lax.dot_general(a, b, (((1,), (1,)), ((), ())), preferred_element_type=F32)


def nn(a, b):
    return lax.dot_general(a, b, (((1,), (0,)), ((), ())), preferred_element_type=F32)


def tn(a, b):
    return lax.dot_general(a, b, (((0,), (0,)), ((), ())), preferred_element_type=F32)


def head_span(h):
    lo = HEAD * h
    t0 = lo // 128 * 128
    t1 = -(-(lo + HEAD) // 128) * 128
    return lo, t0, t1


def masked(x, h):
    lo, t0, t1 = head_span(h)
    cols = lax.broadcasted_iota(jnp.int32, (ROWS, t1 - t0), 1) + t0
    return jnp.where((cols >= lo) & (cols < lo + HEAD), x, jnp.zeros_like(x))


def add_head(acc, h, value):
    lo, t0, t1 = head_span(h)
    for t in range(t0, t1, 128):
        part = value[:, t - t0 : t - t0 + 128]
        if h > 0 and t < -(-lo // 128) * 128 and lo % 128 != 0 and t <= lo:
            acc[:, t : t + 128] += part
        else:
            acc[:, t : t + 128] = part


def kernel(
    patches, cot, win_hbm, gain_hbm, wq_hbm, wo_hbm,
    act, gin, out_q, out_o, out_gain,
    wq, wo, win, gain, hbuf, gbuf, hout, gout, pacc, dacc, packed, pt32, ptb, att, acc, acc2, acc3,
    datt, dp, lifted, rs,
    ngt, atg, dpt, gt32, gperm, dpg, gpg, dgain, dgrecv, dgz, dgzrecv,
    rq, ro, sq, so, zq, zo, fin, finrecv,
    w_sem, in_sem, o_sem, hs, hr, gs, gr, ns, nr, as_, ar, ds, dr, ps, pr, vs, vr, us, ur, qs, qr, os_, or_, fs, fr,
):
    s = lax.axis_index("section")
    m = lax.axis_index("mp")
    z = lax.axis_index("dp")

    def cols_of(j):
        return pl.ds(j * CW, CW)

    def load_patches(j):
        return pltpu.make_async_copy(patches.at[:, cols_of(j)], hbuf.at[j], in_sem.at[j])

    def load_cot(j):
        return pltpu.make_async_copy(cot.at[:, cols_of(j)], gbuf.at[j], in_sem.at[j])

    def load_wq(j):
        return pltpu.make_async_copy(wq_hbm.at[cols_of(j)], wq.at[cols_of(j)], w_sem.at[j])

    load_wo = pltpu.make_async_copy(wo_hbm, wo, w_sem.at[5])
    load_gain = pltpu.make_async_copy(gain_hbm, gain, w_sem.at[6])
    load_win = pltpu.make_async_copy(win_hbm, win, w_sem.at[7])

    load_gain.start()

    @pl.when(s == 0)
    def _():
        for j in range(CHUNKS):
            load_patches(j).start()

    for j in range(CHUNKS):
        load_wq(j).start()
    load_win.start()
    load_wo.start()

    @pl.when(s == NS - 1)
    def _():
        for j in range(CHUNKS):
            load_cot(j).start()

    barrier = pltpu.get_barrier_semaphore()
    for d in range(1, NM):
        pl.semaphore_signal(barrier, inc=1, device_id={"mp": lax.rem(m + d, NM)}, device_id_type=MESH)
    for d in range(1, NZ):
        pl.semaphore_signal(barrier, inc=1, device_id={"dp": lax.rem(z + d, NZ)}, device_id_type=MESH)
    for d in (1, NS - 1):
        pl.semaphore_signal(barrier, inc=1, device_id={"section": lax.rem(s + d, NS)}, device_id_type=MESH)

    dpt[3 * HW : 2048, :] = jnp.zeros((2048 - 3 * HW, ROWS), BF16)
    gt32[VD : VD + 32, :] = jnp.zeros((32, ROWS), F32)

    def remote(src, dst, ssem, rsem, where):
        return pltpu.make_async_remote_copy(
            src_ref=src, dst_ref=dst, send_sem=ssem, recv_sem=rsem, device_id=where, device_id_type=MESH
        )

    def hop_forward(j):
        return remote(hout.at[j], hbuf.at[j], hs.at[j], hr.at[j], {"section": lax.rem(s + 1, NS)})

    def hop_back(j):
        return remote(gout.at[j], gbuf.at[j], gs.at[j], gr.at[j], {"section": lax.rem(s + NS - 1, NS)})

    def mp_lanes(i):
        return pl.ds(pl.multiple_of(i * ROWS, ROWS), ROWS)

    def fold(x):
        return x[:, 0:128] + x[:, 128:256]

    load_gain.wait()
    squares = jnp.zeros((ROWS, 128), F32)
    for j in range(CHUNKS):

        @pl.when(s == 0)
        def _():
            load_patches(j).wait()

        @pl.when(s > 0)
        def _():
            hop_forward(j).wait_recv()

        load_wq(j).wait()
        wide = hbuf[j].astype(F32)
        squares = squares + fold(wide * wide)
        scaled = (wide * gain[:, j * CW : (j + 1) * CW]).astype(BF16)
        for i in range(3):
            part = nn(scaled, wq[j * CW : (j + 1) * CW, i * HW : (i + 1) * HW])
            if j == 0:
                pacc[:, i * HW : (i + 1) * HW] = part
            else:
                pacc[:, i * HW : (i + 1) * HW] += part
    spread = lax.rsqrt(jnp.sum(squares, axis=-1, keepdims=True) * (1.0 / VD) + 1e-6)
    rs[...] = spread
    packed[...] = (pacc[...] * spread).astype(BF16)
    load_win.wait()
    ids = jnp.broadcast_to(win[...].astype(F32), (ROWS, ROWS))
    same = ids.T == ids

    for h in range(HEADS):
        lo, t0, t1 = head_span(h)
        q = packed[:, t0:t1]
        k = masked(packed[:, HW + t0 : HW + t1], h)
        scores = nt(k, q) * SCALE
        scores = jnp.where(same, scores, -1e30)
        top = jnp.max(scores, axis=0, keepdims=True)
        e = jnp.exp(scores - top)
        p = e / jnp.sum(e, axis=0, keepdims=True)
        pt32[h] = p
        ptb[h] = p.astype(BF16)
    for h in range(HEADS):
        lo, t0, t1 = head_span(h)
        v = masked(packed[:, 2 * HW + t0 : 2 * HW + t1], h)
        add_head(acc, h, tn(ptb[h], v))
    att[...] = acc[...].astype(BF16)
    load_wo.wait()
    pl.semaphore_wait(barrier, (NM - 1) + (NZ - 1) + 2)

    def project(j):
        hout[j] = (hbuf[j].astype(F32) + nn(att[...], wo[:, j * CW : (j + 1) * CW])).astype(BF16)

    chip = m // 2
    core = lax.rem(m, 2)
    sibling = chip * 2 + 1 - core

    def gather_copy(which, slot, i, to):
        lanes = mp_lanes(slot)
        if which == 0:
            return remote(ngt.at[:, lanes], ngt.at[:, lanes], ns.at[i], nr.at[i], {"mp": to})
        return remote(atg.at[lanes, :], atg.at[lanes, :], as_.at[i], ar.at[i], {"mp": to})

    def across(d):
        return lax.rem(chip + d, NM // 2) * 2 + core

    def gather_start():
        for j in range(CHUNKS):
            wide = hbuf[j].astype(F32) * rs[...] * gain[:, j * CW : (j + 1) * CW]
            ngt[j * CW : (j + 1) * CW, mp_lanes(m)] = wide.astype(BF16).T
        atg[mp_lanes(m), :] = att[...]
        for w in range(2):
            for d in range(1, NM // 2):
                gather_copy(w, m, d, across(d)).start()
            gather_copy(w, m, 0, sibling).start()

    def gather_forward():
        for d in range(1, NM // 2):
            source = across(NM // 2 - d)
            for w in range(2):
                gather_copy(w, source, d, across(d)).wait_recv()
                gather_copy(w, source, NM // 2 - 1 + d, sibling).start()

    def gather_finish(w):
        gather_copy(w, sibling, 0, sibling).wait_recv()
        for d in range(1, NM // 2):
            source = lax.rem(chip + NM // 2 - d, NM // 2) * 2 + 1 - core
            gather_copy(w, source, NM // 2 - 1 + d, sibling).wait_recv()

    @pl.when(s < NS - 1)
    def _():
        for j in range(CHUNKS):
            project(j)
            hop_forward(j).start()

    gather_start()

    @pl.when(s < NS - 2)
    def _():
        gather_forward()

    def column_copy(which, d):
        to = lax.rem(m + d, NM)
        rows = pl.ds(pl.multiple_of(to * 256, 256), 256)
        lanes = mp_lanes(m)
        if which == 0:
            return remote(dpt.at[rows], dpg.at[:, lanes], ds.at[d], dr.at[d], {"mp": to})
        return remote(gperm.at[rows], gpg.at[:, lanes], ps.at[d], pr.at[d], {"mp": to})

    def columns_q():
        dpt[0 : 3 * HW, :] = dp[...].T
        for d in range(1, NM):
            column_copy(0, d).start()
        dpg[:, mp_lanes(m)] = dpt[pl.ds(pl.multiple_of(m * 256, 256), 256), :]

    def turn_g(j):
        gt32[j * CW : (j + 1) * CW, :] = gbuf[j].astype(F32).T

    def columns_g():
        for i in range(NM):
            for j in range(NZ):
                first = FR * (NM * j + i)
                gperm[i * 256 + j * 32 : i * 256 + j * 32 + 32, :] = gt32[first : first + 32, :].astype(BF16)
        for d in range(1, NM):
            column_copy(1, d).start()
        gpg[:, mp_lanes(m)] = gperm[pl.ds(pl.multiple_of(m * 256, 256), 256), :]

    for j in range(CHUNKS):

        @pl.when(s == NS - 1)
        def _():
            load_cot(j).wait()

        @pl.when(s < NS - 1)
        def _():
            hop_back(j).wait_recv()

        part = nt(gbuf[j], wo[:, j * CW : (j + 1) * CW])
        if j == 0:
            dacc[...] = part
        else:
            dacc[...] += part

        @pl.when(s == 0)
        def _():
            turn_g(j)

    datt[...] = dacc[...].astype(BF16)

    @pl.when(s == 0)
    def _():
        columns_g()

    for h in range(HEADS):
        lo, t0, t1 = head_span(h)
        q = masked(packed[:, t0:t1], h)
        k = masked(packed[:, HW + t0 : HW + t1], h)
        v = masked(packed[:, 2 * HW + t0 : 2 * HW + t1], h)
        da = datt[:, t0:t1]
        dprob = nt(v, da).astype(BF16).astype(F32)
        p = pt32[h]
        dsc = p * (dprob - jnp.sum(p * dprob, axis=0, keepdims=True))
        dsc = (dsc * SCALE).astype(BF16)
        add_head(acc, h, tn(dsc, k))
        add_head(acc2, h, nn(dsc, q))
        add_head(acc3, h, nn(ptb[h], masked(da, h)))
    dp[:, 0:HW] = acc[...].astype(BF16)
    dp[:, HW : 2 * HW] = acc2[...].astype(BF16)
    dp[:, 2 * HW : 3 * HW] = acc3[...].astype(BF16)

    @pl.when(s == 0)
    def _():
        columns_q()

    inner = jnp.zeros((ROWS, 128), F32)
    for j in range(CHUNKS):
        dn = nt(dp[...], wq[j * CW : (j + 1) * CW, :]).astype(BF16).astype(F32)
        wide = hbuf[j].astype(F32)
        up = dn * gain[:, j * CW : (j + 1) * CW]
        lifted[j] = up
        inner = inner + fold(up * wide)
        dgain[0, :, j * CW : (j + 1) * CW] = jnp.sum(dn * (wide * rs[...]), axis=0, keepdims=True)
    spread = rs[...]
    pull = jnp.sum(inner, axis=-1, keepdims=True) * (1.0 / VD) * (spread * spread * spread)
    for j in range(CHUNKS):
        back = gbuf[j].astype(F32) + spread * lifted[j] - hbuf[j].astype(F32) * pull
        gout[j] = back.astype(BF16)

        @pl.when(s > 0)
        def _():
            hop_back(j).start()

    def store_act(j):
        return pltpu.make_async_copy(hout.at[j], act.at[:, cols_of(j)], o_sem.at[j])

    def store_gin(j):
        return pltpu.make_async_copy(gout.at[j], gin.at[:, cols_of(j)], o_sem.at[CHUNKS + j])

    for j in range(CHUNKS):
        store_gin(j).start()

    @pl.when(s > 0)
    def _():
        columns_q()
        for j in range(CHUNKS):
            turn_g(j)
        columns_g()

    @pl.when(s == NS - 1)
    def _():
        for j in range(CHUNKS):
            project(j)

    @pl.when(s >= NS - 2)
    def _():
        gather_forward()

    for j in range(CHUNKS):
        store_act(j).start()

    def gain_mp(d):
        return remote(dgain.at[0], dgrecv.at[d], vs.at[d], vr.at[d], {"mp": lax.rem(m + d, NM)})

    def gain_dp(d):
        return remote(dgz.at[0], dgzrecv.at[d], us.at[d], ur.at[d], {"dp": lax.rem(z + d, NZ)})

    for d in range(1, NM):
        gain_mp(d).start()

    def chunk_q(k):
        rows = pl.ds(pl.multiple_of(k * ZR, 16), ZR)
        return nt(ngt[rows, :], dpg[...])

    def chunk_o(k):
        rows = pl.ds(pl.multiple_of(k * 32, 32), 32)
        return nn(gpg[rows, :], atg[...])

    steps = (NZ - 1, 1, NZ - 2, 2, NZ - 1, 1, NZ - 2, 2)
    owners = (NZ - 3, 3, 4, 4, NZ - 1, 1, NZ - 2, 2)

    def peer(i):
        return {"dp": lax.rem(z + steps[i], NZ)}

    def tree_q(i):
        if i == 2 or i == 3:
            half = pl.ds(0, ZR // 2)
            return remote(sq.at[i, half], zq.at[i, half], qs.at[i], qr.at[i], peer(i))
        return remote(sq.at[i], zq.at[i], qs.at[i], qr.at[i], peer(i))

    def tree_o(i):
        if i == 2 or i == 3:
            half = pl.ds(0, 16)
            return remote(so.at[i, half], zo.at[i, half], os_.at[i], or_.at[i], peer(i))
        return remote(so.at[i], zo.at[i], os_.at[i], or_.at[i], peer(i))

    def whose(i):
        return lax.rem(z + owners[i], NZ)

    def leaf(i, chunk, buf, copy, rows):
        if i == 2:
            value = chunk(whose(2)).astype(BF16)
            buf[2, 0 : rows // 2] = value[0 : rows // 2]
            buf[3, 0 : rows // 2] = value[rows // 2 : rows]
            copy(2).start()
            copy(3).start()
        else:
            buf[i] = chunk(whose(i)).astype(BF16)
            copy(i).start()

    def branch(i, chunk, buf, got, copy, rows, hold):
        hold[...] = chunk(whose(i))
        copy(i - 6).wait_recv()
        hold[...] += got[i - 6].astype(F32)
        copy(i - 4).wait_recv()
        if i == 6:
            hold[0 : rows // 2] += got[2, 0 : rows // 2].astype(F32)
        else:
            hold[rows // 2 : rows] += got[3, 0 : rows // 2].astype(F32)
        buf[i] = hold[...].astype(BF16)
        copy(i).start()

    gather_finish(1)
    for d in range(1, NM):
        column_copy(1, d).wait_recv()
    for i in (2, 0, 1, 4, 5):
        leaf(i, chunk_o, so, tree_o, 32)

    gather_finish(0)
    for d in range(1, NM):
        column_copy(0, d).wait_recv()
    for i in (2, 0, 1):
        leaf(i, chunk_q, sq, tree_q, ZR)

    for i in (6, 7):
        branch(i, chunk_o, so, zo, tree_o, 32, ro)
    for i in (4, 5):
        leaf(i, chunk_q, sq, tree_q, ZR)

    sum_gain = dgain[0]
    for d in range(1, NM):
        gain_mp(d).wait_recv()
        sum_gain = sum_gain + dgrecv[d]
    dgz[0] = sum_gain
    for d in range(1, NZ):
        gain_dp(d).start()

    for i in (6, 7):
        branch(i, chunk_q, sq, zq, tree_q, ZR, rq.at[0:ZR])

    ro[...] = chunk_o(z)
    for i in (4, 5, 6, 7):
        tree_o(i).wait_recv()
        ro[...] += zo[i].astype(F32)
    out_o[:, 0, :] = ro[0:FR, :]

    rq[0:ZR, :] = chunk_q(z)
    for i in (4, 5, 6, 7):
        tree_q(i).wait_recv()
        rq[0:ZR, :] += zq[i].astype(F32)

    def piece(d):
        return remote(fin.at[lax.rem(m + d, NM)], finrecv.at[m], fs.at[d], fr.at[d], {"mp": lax.rem(m + d, NM)})

    for i in range(NM):
        if FR * i + 24 <= ZR:
            fin[i] = rq[FR * i : FR * i + 24, :]
        else:
            fin[i, 0:FR] = rq[FR * i : FR * i + FR, :]
            fin[i, FR:24] = jnp.zeros((24 - FR, 256), F32)
    for d in range(1, NM):
        piece(d).start()
    finrecv[m] = fin[m]

    sum_gain = dgz[0]
    for d in range(1, NZ):
        gain_dp(d).wait_recv()
        sum_gain = sum_gain + dgzrecv[d]
    out_gain[...] = sum_gain

    @pl.when(s < NS - 1)
    def _():
        for j in range(CHUNKS):
            hop_forward(j).wait_send()

    @pl.when(s > 0)
    def _():
        for j in range(CHUNKS):
            hop_back(j).wait_send()

    for i in range(NM - 1):
        for w in range(2):
            gather_copy(w, m, i, sibling).wait_send()
    for d in range(1, NM):
        for w in range(2):
            column_copy(w, d).wait_send()
        gain_mp(d).wait_send()
    for d in range(1, NZ):
        gain_dp(d).wait_send()
    for i in range(8):
        tree_q(i).wait_send()
        tree_o(i).wait_send()
    for j in range(CHUNKS):
        store_act(j).wait()
        store_gin(j).wait()

    for d in range(1, NM):
        source = lax.rem(m + NM - d, NM)
        remote(fin.at[source], finrecv.at[source], fs.at[d], fr.at[d], {"mp": source}).wait_recv()
    for i in range(NM):
        wide = min(256, 3 * HW - 256 * i)
        out_q[:, 0, 256 * i : 256 * i + wide] = finrecv[i, 0:FR, 0:wide]
    for d in range(1, NM):
        piece(d).wait_send()


def finish(act, gin, out_q, out_o, gain, act2, gin2, out_q2, out_o2, gain2, a, b, c, d, sem):
    there = ((act, a), (gin, b), (out_q, c), (out_o, d))
    back = ((a, act2), (b, gin2), (c, out_q2), (d, out_o2))
    reads = [pltpu.make_async_copy(x, y, sem.at[i]) for i, (x, y) in enumerate(there)]
    writes = [pltpu.make_async_copy(x, y, sem.at[4 + i]) for i, (x, y) in enumerate(back)]
    for r in reads:
        r.start()
    place = (lax.axis_index("dp") * NM + lax.axis_index("mp")) * FR
    rows = jnp.broadcast_to(gain[...], (8, VD))
    gain2[...] = pltpu.roll(rows, lax.rem(VD - place, VD), 1)[0:1, 0:FR]
    for r, w in zip(reads, writes):
        r.wait()
        w.start()
    for w in writes:
        w.wait()


def on_device(patches, windows, gain, w_qkv, w_out, cotangent):
    vmem = pl.BlockSpec(memory_space=pltpu.VMEM)
    hbm = pl.BlockSpec(memory_space=pl.ANY)
    dma = pltpu.SemaphoreType.DMA
    scratch = [
        pltpu.VMEM((VD, 3 * HW), BF16),
        pltpu.VMEM((HW, VD), BF16),
        pltpu.VMEM((1, ROWS), jnp.int32),
        pltpu.VMEM((1, VD), F32),
        pltpu.VMEM((CHUNKS, ROWS, CW), BF16),
        pltpu.VMEM((CHUNKS, ROWS, CW), BF16),
        pltpu.VMEM((CHUNKS, ROWS, CW), BF16),
        pltpu.VMEM((CHUNKS, ROWS, CW), BF16),
        pltpu.VMEM((ROWS, 3 * HW), F32),
        pltpu.VMEM((ROWS, HW), F32),
        pltpu.VMEM((ROWS, 3 * HW), BF16),
        pltpu.VMEM((HEADS, ROWS, ROWS), F32),
        pltpu.VMEM((HEADS, ROWS, ROWS), BF16),
        pltpu.VMEM((ROWS, HW), BF16),
        pltpu.VMEM((ROWS, HW), F32),
        pltpu.VMEM((ROWS, HW), F32),
        pltpu.VMEM((ROWS, HW), F32),
        pltpu.VMEM((ROWS, HW), BF16),
        pltpu.VMEM((ROWS, 3 * HW), BF16),
        pltpu.VMEM((CHUNKS, ROWS, CW), F32),
        pltpu.VMEM((ROWS, 1), F32),
        pltpu.VMEM((VD, NM * ROWS), BF16),
        pltpu.VMEM((NM * ROWS, HW), BF16),
        pltpu.VMEM((2048, ROWS), BF16),
        pltpu.VMEM((VD + 32, ROWS), F32),
        pltpu.VMEM((2048, ROWS), BF16),
        pltpu.VMEM((256, NM * ROWS), BF16),
        pltpu.VMEM((256, NM * ROWS), BF16),
        pltpu.VMEM((1, 1, VD), F32),
        pltpu.VMEM((NM, 1, VD), F32),
        pltpu.VMEM((1, 1, VD), F32),
        pltpu.VMEM((NZ, 1, VD), F32),
        pltpu.VMEM((ZR, 256), F32),
        pltpu.VMEM((32, HW), F32),
        pltpu.VMEM((8, ZR, 256), BF16),
        pltpu.VMEM((8, 32, HW), BF16),
        pltpu.VMEM((8, ZR, 256), BF16),
        pltpu.VMEM((8, 32, HW), BF16),
        pltpu.VMEM((NM, 24, 256), F32),
        pltpu.VMEM((NM, 24, 256), F32),
        dma((8,)), dma((CHUNKS,)), dma((2 * CHUNKS,)),
        dma((CHUNKS,)), dma((CHUNKS,)), dma((CHUNKS,)), dma((CHUNKS,)),
    ] + [dma((8,)) for _ in range(18)]
    shapes = (
        jax.ShapeDtypeStruct((ROWS, VD), BF16),
        jax.ShapeDtypeStruct((ROWS, VD), BF16),
        jax.ShapeDtypeStruct((FR, 1, 3 * HW), F32),
        jax.ShapeDtypeStruct((FR, 1, HW), F32),
        jax.ShapeDtypeStruct((1, VD), F32),
    )
    results = pl.pallas_call(
        kernel,
        out_shape=shapes,
        in_specs=[hbm] * 6,
        out_specs=(hbm, hbm, vmem, vmem, vmem),
        scratch_shapes=scratch,
        compiler_params=pltpu.CompilerParams(
            collective_id=0, has_side_effects=True, vmem_limit_bytes=60 * 1024 * 1024
        ),
    )(patches[0], cotangent[0], windows, gain, w_qkv[0], w_out[0])
    act, gin, out_q, out_o, own_gain = pl.pallas_call(
        finish,
        out_shape=shapes[:4] + (jax.ShapeDtypeStruct((1, FR), F32),),
        in_specs=[hbm] * 4 + [vmem],
        out_specs=(hbm,) * 4 + (vmem,),
        scratch_shapes=[pltpu.VMEM(x.shape, x.dtype) for x in shapes[:4]] + [dma((8,))],
        compiler_params=pltpu.CompilerParams(vmem_limit_bytes=60 * 1024 * 1024),
    )(*results)
    return (
        act[None, None],
        gin[None, None],
        out_q.transpose(1, 0, 2),
        out_o.transpose(1, 2, 0),
        own_gain,
    )


def solution(mesh):
    in_specs = (
        P(None, ("dp", "mp"), None),
        P(None, ("dp", "mp")),
        P("section", None),
        P("section", None, None),
        P("section", None, None),
        P(None, ("dp", "mp"), None),
    )
    out_specs = (
        P("section", None, ("dp", "mp"), None),
        P("section", None, ("dp", "mp"), None),
        P("section", ("dp", "mp"), None),
        P("section", None, ("dp", "mp")),
        P("section", ("dp", "mp")),
    )
    return jax.shard_map(
        on_device, mesh=mesh, in_specs=in_specs, out_specs=out_specs, check_vma=False
    )
```

time: 129 us -> 106 us (0.82)
  Pallas kernels: 119 us -> 105 us
  local copies, waits for them, and re-layouts: 9.1 us -> 0 us
    pallas_call x1 -> x2, Pallas kernels: 119 us -> 105 us  [the longest x1 102 us: on_device(): pl.pallas_call(kernel, out_shape=shapes, in_specs=[hbm] * 6, out_specs=(h...]
    unnamed x14 -> x0, local copies, waits for them, and re-layouts: 7.75 us -> none
where the time goes in v2:
time: 106 us
  Pallas kernels  105 us (99%)
    pallas_call x1, Pallas kernels, on_device(): pl.pallas_call(kernel, out_shape=shapes, in_specs=[hbm] * 6, out_specs=(h...  102 us
    pallas_call x1, Pallas kernels, on_device(): pl.pallas_call(finish, out_shape=shapes[:4] + (jax.ShapeDtypeStruct((1, F...  3.13 us

profile of v2, /device:TPU:1, one launch (start us, length us, event | category | flops | bytes accessed | tf_op | source)
XLA Modules:
  0.0 106.0 jit_solution(17716329583565123220)
XLA Ops:
  0.6 102.2 %shard_map.101 = (bf16[128,1280]{1,0:T(8,128)(2,1)}, bf16[128,1280]{1,0:T(8,128)(2,1)}, f32[20,1,1920]{2,1,0:T(1,128)}, f32[20,1,640]{2,1,0:T(1,128)}, f32[1,1280]{1,0:T(1,128)}) custom-call(bf16[128,1280]{1,0:T(8,128)(2,1)} %bitcast.10, bf16[128,1280]{1,0:T(8,128)(2,1)} %bitcast.11, s32[1,128]{1,0:T(1,128)} %win_hbm.1, f32[1,1280]{1,0:T(1,128)} %gain_hbm.1, ...), custom_call_target="tpu_custom_call" | custom-call | tf_op jit(solution)/shard_map/pallas_call | solution.py:580
  102.8 3.1 %shard_map.102 = (bf16[128,1280]{1,0:T(8,128)(2,1)}, bf16[128,1280]{1,0:T(8,128)(2,1)}, f32[20,1,1920]{2,1,0:T(1,128)}, f32[20,1,640]{2,1,0:T(1,128)}, f32[1,20]{1,0:T(1,128)}) custom-call(bf16[128,1280]{1,0:T(8,128)(2,1)} %get-tuple-element.15.act, bf16[128,1280]{1,0:T(8,128)(2,1)} %get-tuple-element.16.gin, f32[20,1,1920]{2,1,0:T(1,128)} %get-tuple-element.17.out_q, ...), custom_call_target="tpu_custom_call" | custom-call | tf_op jit(solution)/shard_map/pallas_call | solution.py:590

commit v3 on v2

--- a/solution.py
+++ b/solution.py
@@ -35,35 +35,46 @@
     return lax.dot_general(a, b, (((0,), (0,)), ((), ())), preferred_element_type=F32)
 
 
-def head_span(h):
-    lo = HEAD * h
-    t0 = lo // 128 * 128
-    t1 = -(-(lo + HEAD) // 128) * 128
-    return lo, t0, t1
-
-
-def masked(x, h):
-    lo, t0, t1 = head_span(h)
-    cols = lax.broadcasted_iota(jnp.int32, (ROWS, t1 - t0), 1) + t0
-    return jnp.where((cols >= lo) & (cols < lo + HEAD), x, jnp.zeros_like(x))
-
-
-def add_head(acc, h, value):
-    lo, t0, t1 = head_span(h)
-    for t in range(t0, t1, 128):
-        part = value[:, t - t0 : t - t0 + 128]
-        if h > 0 and t < -(-lo // 128) * 128 and lo % 128 != 0 and t <= lo:
-            acc[:, t : t + 128] += part
-        else:
-            acc[:, t : t + 128] = part
+def tiles_of(h):
+    return range(HEAD * h // 128, -(-(HEAD * h + HEAD) // 128))
+
+
+def heads_of(t):
+    return [h for h in range(HEADS) if t in tiles_of(h)]
+
+
+PAIRS = [(t, h) for t in range(HW // 128) for h in heads_of(t)]
+
+
+def pair_rows(t):
+    first = PAIRS.index((t, heads_of(t)[0]))
+    return slice(first * ROWS, (first + len(heads_of(t))) * ROWS)
+
+
+def head_rows(t):
+    heads = heads_of(t)
+    return slice(heads[0] * ROWS, (heads[-1] + 1) * ROWS)
+
+
+def gathered(stack, h):
+    parts = []
+    for t in tiles_of(h):
+        i = PAIRS.index((t, h))
+        parts.append(stack[i * ROWS : (i + 1) * ROWS, :])
+    return parts[0] if len(parts) == 1 else jnp.concatenate(parts, axis=1)
+
+
+def span(h):
+    tiles = tiles_of(h)
+    return tiles[0] * 128, tiles[-1] * 128 + 128
 
 
 def kernel(
     patches, cot, win_hbm, gain_hbm, wq_hbm, wo_hbm,
     act, gin, out_q, out_o, out_gain,
-    wq, wo, win, gain, hbuf, gbuf, hout, gout, pacc, dacc, packed, pt32, ptb, att, acc, acc2, acc3,
-    datt, dp, lifted, rs,
-    ngt, atg, dpt, gt32, gperm, dpg, gpg, dgain, dgrecv, dgz, dgzrecv,
+    wq, wo, win, gain, hbuf, gbuf, hout, gout, pacc, dacc, packed, pt32, ptb, ptl, att, mk, qm, km, vm, dam, dsr, dsl,
+    datt, dp, lifted, rs, wqt, oq, oo,
+    ngt, atg, gt32, gperm, dpg, gpg, dgain, dgrecv, dgz, dgzrecv,
     rq, ro, sq, so, zq, zo, fin, finrecv,
     w_sem, in_sem, o_sem, hs, hr, gs, gr, ns, nr, as_, ar, ds, dr, ps, pr, vs, vr, us, ur, qs, qr, os_, or_, fs, fr,
 ):
@@ -112,7 +123,12 @@
     for d in (1, NS - 1):
         pl.semaphore_signal(barrier, inc=1, device_id={"section": lax.rem(s + d, NS)}, device_id_type=MESH)
 
-    dpt[3 * HW : 2048, :] = jnp.zeros((2048 - 3 * HW, ROWS), BF16)
+    dp[:, 3 * HW : 2048] = jnp.zeros((ROWS, 2048 - 3 * HW), BF16)
+    rq[ZR : ZR + 32, :] = jnp.zeros((32, 256), F32)
+    for i, (t, h) in enumerate(PAIRS):
+        cols = lax.broadcasted_iota(jnp.int32, (ROWS, 128), 1) + t * 128
+        inside = (cols >= HEAD * h) & (cols < HEAD * h + HEAD)
+        mk[i] = jnp.where(inside, 1.0, 0.0).astype(BF16)
     gt32[VD : VD + 32, :] = jnp.zeros((32, ROWS), F32)
 
     def remote(src, dst, ssem, rsem, where):
@@ -133,6 +149,12 @@
         return x[:, 0:128] + x[:, 128:256]
 
     load_gain.wait()
+    @pl.when(s >= 2)
+    def _():
+        for j in range(CHUNKS):
+            load_wq(j).wait()
+            wqt[:, j * CW : (j + 1) * CW] = wq[j * CW : (j + 1) * CW, :].T
+
     squares = jnp.zeros((ROWS, 128), F32)
     for j in range(CHUNKS):
 
@@ -144,7 +166,10 @@
         def _():
             hop_forward(j).wait_recv()
 
-        load_wq(j).wait()
+        @pl.when(s < 2)
+        def _():
+            load_wq(j).wait()
+
         wide = hbuf[j].astype(F32)
         squares = squares + fold(wide * wide)
         scaled = (wide * gain[:, j * CW : (j + 1) * CW]).astype(BF16)
@@ -161,22 +186,21 @@
     ids = jnp.broadcast_to(win[...].astype(F32), (ROWS, ROWS))
     same = ids.T == ids
 
+    for i, (t, h) in enumerate(PAIRS):
+        rows = slice(i * ROWS, (i + 1) * ROWS)
+        km[rows, :] = packed[:, HW + t * 128 : HW + t * 128 + 128] * mk[i]
+        vm[rows, :] = packed[:, 2 * HW + t * 128 : 2 * HW + t * 128 + 128] * mk[i]
     for h in range(HEADS):
-        lo, t0, t1 = head_span(h)
-        q = packed[:, t0:t1]
-        k = masked(packed[:, HW + t0 : HW + t1], h)
-        scores = nt(k, q) * SCALE
+        t0, t1 = span(h)
+        scores = nt(gathered(km, h), packed[:, t0:t1]) * SCALE
         scores = jnp.where(same, scores, -1e30)
         top = jnp.max(scores, axis=0, keepdims=True)
         e = jnp.exp(scores - top)
         p = e / jnp.sum(e, axis=0, keepdims=True)
         pt32[h] = p
-        ptb[h] = p.astype(BF16)
-    for h in range(HEADS):
-        lo, t0, t1 = head_span(h)
-        v = masked(packed[:, 2 * HW + t0 : 2 * HW + t1], h)
-        add_head(acc, h, tn(ptb[h], v))
-    att[...] = acc[...].astype(BF16)
+        ptb[h * ROWS : (h + 1) * ROWS, :] = p.astype(BF16)
+    for t in range(HW // 128):
+        att[:, t * 128 : t * 128 + 128] = tn(ptb[head_rows(t), :], vm[pair_rows(t), :]).astype(BF16)
     load_wo.wait()
     pl.semaphore_wait(barrier, (NM - 1) + (NZ - 1) + 2)
 
@@ -231,19 +255,31 @@
     def _():
         gather_forward()
 
+    def turn_weights():
+        for j in range(CHUNKS):
+            wqt[:, j * CW : (j + 1) * CW] = wq[j * CW : (j + 1) * CW, :].T
+
+    @pl.when(s < 2)
+    def _():
+        turn_weights()
+
+    for i, (t, h) in enumerate(PAIRS):
+        qm[i * ROWS : (i + 1) * ROWS, :] = packed[:, t * 128 : t * 128 + 128] * mk[i]
+    for h in range(HEADS):
+        ptl[:, h * ROWS : (h + 1) * ROWS] = ptb[h * ROWS : (h + 1) * ROWS, :]
+
     def column_copy(which, d):
         to = lax.rem(m + d, NM)
         rows = pl.ds(pl.multiple_of(to * 256, 256), 256)
         lanes = mp_lanes(m)
         if which == 0:
-            return remote(dpt.at[rows], dpg.at[:, lanes], ds.at[d], dr.at[d], {"mp": to})
+            return remote(dp.at[:, rows], dpg.at[lanes, :], ds.at[d], dr.at[d], {"mp": to})
         return remote(gperm.at[rows], gpg.at[:, lanes], ps.at[d], pr.at[d], {"mp": to})
 
     def columns_q():
-        dpt[0 : 3 * HW, :] = dp[...].T
         for d in range(1, NM):
             column_copy(0, d).start()
-        dpg[:, mp_lanes(m)] = dpt[pl.ds(pl.multiple_of(m * 256, 256), 256), :]
+        dpg[mp_lanes(m), :] = dp[:, pl.ds(pl.multiple_of(m * 256, 256), 256)]
 
     def turn_g(j):
         gt32[j * CW : (j + 1) * CW, :] = gbuf[j].astype(F32).T
@@ -283,22 +319,23 @@
     def _():
         columns_g()
 
+    for i, (t, h) in enumerate(PAIRS):
+        dam[i * ROWS : (i + 1) * ROWS, :] = datt[:, t * 128 : t * 128 + 128] * mk[i]
     for h in range(HEADS):
-        lo, t0, t1 = head_span(h)
-        q = masked(packed[:, t0:t1], h)
-        k = masked(packed[:, HW + t0 : HW + t1], h)
-        v = masked(packed[:, 2 * HW + t0 : 2 * HW + t1], h)
-        da = datt[:, t0:t1]
-        dprob = nt(v, da).astype(BF16).astype(F32)
+        t0, t1 = span(h)
+        dprob = nt(gathered(vm, h), datt[:, t0:t1]).astype(BF16).astype(F32)
         p = pt32[h]
         dsc = p * (dprob - jnp.sum(p * dprob, axis=0, keepdims=True))
         dsc = (dsc * SCALE).astype(BF16)
-        add_head(acc, h, tn(dsc, k))
-        add_head(acc2, h, nn(dsc, q))
-        add_head(acc3, h, nn(ptb[h], masked(da, h)))
-    dp[:, 0:HW] = acc[...].astype(BF16)
-    dp[:, HW : 2 * HW] = acc2[...].astype(BF16)
-    dp[:, 2 * HW : 3 * HW] = acc3[...].astype(BF16)
+        dsr[h * ROWS : (h + 1) * ROWS, :] = dsc
+        dsl[:, h * ROWS : (h + 1) * ROWS] = dsc
+    for t in range(HW // 128):
+        c = t * 128
+        dp[:, 2 * HW + c : 2 * HW + c + 128] = nn(ptl[:, head_rows(t)], dam[pair_rows(t), :]).astype(BF16)
+    for t in range(HW // 128):
+        c = t * 128
+        dp[:, HW + c : HW + c + 128] = nn(dsl[:, head_rows(t)], qm[pair_rows(t), :]).astype(BF16)
+        dp[:, c : c + 128] = tn(dsr[head_rows(t), :], km[pair_rows(t), :]).astype(BF16)
 
     @pl.when(s == 0)
     def _():
@@ -306,7 +343,7 @@
 
     inner = jnp.zeros((ROWS, 128), F32)
     for j in range(CHUNKS):
-        dn = nt(dp[...], wq[j * CW : (j + 1) * CW, :]).astype(BF16).astype(F32)
+        dn = nn(dp[:, 0 : 3 * HW], wqt[:, j * CW : (j + 1) * CW]).astype(BF16).astype(F32)
         wide = hbuf[j].astype(F32)
         up = dn * gain[:, j * CW : (j + 1) * CW]
         lifted[j] = up
@@ -361,7 +398,7 @@
 
     def chunk_q(k):
         rows = pl.ds(pl.multiple_of(k * ZR, 16), ZR)
-        return nt(ngt[rows, :], dpg[...])
+        return nn(ngt[rows, :], dpg[...])
 
     def chunk_o(k):
         rows = pl.ds(pl.multiple_of(k * 32, 32), 32)
@@ -428,6 +465,9 @@
     for i in (4, 5):
         leaf(i, chunk_q, sq, tree_q, ZR)
 
+    for i in (6, 7):
+        branch(i, chunk_q, sq, zq, tree_q, ZR, rq.at[0:ZR])
+
     sum_gain = dgain[0]
     for d in range(1, NM):
         gain_mp(d).wait_recv()
@@ -436,14 +476,13 @@
     for d in range(1, NZ):
         gain_dp(d).start()
 
-    for i in (6, 7):
-        branch(i, chunk_q, sq, zq, tree_q, ZR, rq.at[0:ZR])
-
     ro[...] = chunk_o(z)
     for i in (4, 5, 6, 7):
         tree_o(i).wait_recv()
         ro[...] += zo[i].astype(F32)
-    out_o[:, 0, :] = ro[0:FR, :]
+    oo[:, 0, :] = ro[0:FR, :]
+    store_o = pltpu.make_async_copy(oo, out_o, o_sem.at[2 * CHUNKS])
+    store_o.start()
 
     rq[0:ZR, :] = chunk_q(z)
     for i in (4, 5, 6, 7):
@@ -454,11 +493,7 @@
         return remote(fin.at[lax.rem(m + d, NM)], finrecv.at[m], fs.at[d], fr.at[d], {"mp": lax.rem(m + d, NM)})
 
     for i in range(NM):
-        if FR * i + 24 <= ZR:
-            fin[i] = rq[FR * i : FR * i + 24, :]
-        else:
-            fin[i, 0:FR] = rq[FR * i : FR * i + FR, :]
-            fin[i, FR:24] = jnp.zeros((24 - FR, 256), F32)
+        fin[i] = rq[FR * i : FR * i + 32, :].astype(BF16)
     for d in range(1, NM):
         piece(d).start()
     finrecv[m] = fin[m]
@@ -467,7 +502,9 @@
     for d in range(1, NZ):
         gain_dp(d).wait_recv()
         sum_gain = sum_gain + dgzrecv[d]
-    out_gain[...] = sum_gain
+    dgz[1] = sum_gain
+    store_gain = pltpu.make_async_copy(dgz.at[1], out_gain, o_sem.at[2 * CHUNKS + 1])
+    store_gain.start()
 
     @pl.when(s < NS - 1)
     def _():
@@ -500,30 +537,35 @@
         remote(fin.at[source], finrecv.at[source], fs.at[d], fr.at[d], {"mp": source}).wait_recv()
     for i in range(NM):
         wide = min(256, 3 * HW - 256 * i)
-        out_q[:, 0, 256 * i : 256 * i + wide] = finrecv[i, 0:FR, 0:wide]
+        oq[:, 0, 256 * i : 256 * i + wide] = finrecv[i, :, 0:wide].astype(F32)[0:FR]
+    store_q = pltpu.make_async_copy(oq, out_q, o_sem.at[2 * CHUNKS + 2])
+    store_q.start()
     for d in range(1, NM):
         piece(d).wait_send()
-
-
-def finish(act, gin, out_q, out_o, gain, act2, gin2, out_q2, out_o2, gain2, a, b, c, d, sem):
-    there = ((act, a), (gin, b), (out_q, c), (out_o, d))
-    back = ((a, act2), (b, gin2), (c, out_q2), (d, out_o2))
+    store_o.wait()
+    store_gain.wait()
+    store_q.wait()
+
+
+def finish(act, gin, out_q, out_o, gain, act2, gin2, out_q2, out_o2, gain2, a, b, c, d, e, f, sem):
+    there = ((gain, e), (act, a), (gin, b), (out_q, c), (out_o, d))
+    back = ((f, gain2), (a, act2), (b, gin2), (c, out_q2), (d, out_o2))
     reads = [pltpu.make_async_copy(x, y, sem.at[i]) for i, (x, y) in enumerate(there)]
-    writes = [pltpu.make_async_copy(x, y, sem.at[4 + i]) for i, (x, y) in enumerate(back)]
+    writes = [pltpu.make_async_copy(x, y, sem.at[5 + i]) for i, (x, y) in enumerate(back)]
     for r in reads:
         r.start()
     place = (lax.axis_index("dp") * NM + lax.axis_index("mp")) * FR
-    rows = jnp.broadcast_to(gain[...], (8, VD))
-    gain2[...] = pltpu.roll(rows, lax.rem(VD - place, VD), 1)[0:1, 0:FR]
-    for r, w in zip(reads, writes):
+    for i, (r, w) in enumerate(zip(reads, writes)):
         r.wait()
+        if i == 0:
+            rows = jnp.broadcast_to(e[...], (8, VD))
+            f[...] = pltpu.roll(rows, lax.rem(VD - place, VD), 1)[0:1, 0:FR]
         w.start()
     for w in writes:
         w.wait()
 
 
 def on_device(patches, windows, gain, w_qkv, w_out, cotangent):
-    vmem = pl.BlockSpec(memory_space=pltpu.VMEM)
     hbm = pl.BlockSpec(memory_space=pl.ANY)
     dma = pltpu.SemaphoreType.DMA
     scratch = [
@@ -539,35 +581,42 @@
         pltpu.VMEM((ROWS, HW), F32),
         pltpu.VMEM((ROWS, 3 * HW), BF16),
         pltpu.VMEM((HEADS, ROWS, ROWS), F32),
-        pltpu.VMEM((HEADS, ROWS, ROWS), BF16),
+        pltpu.VMEM((HEADS * ROWS, ROWS), BF16),
+        pltpu.VMEM((ROWS, HEADS * ROWS), BF16),
         pltpu.VMEM((ROWS, HW), BF16),
-        pltpu.VMEM((ROWS, HW), F32),
-        pltpu.VMEM((ROWS, HW), F32),
-        pltpu.VMEM((ROWS, HW), F32),
+        pltpu.VMEM((len(PAIRS), ROWS, 128), BF16),
+        pltpu.VMEM((len(PAIRS) * ROWS, 128), BF16),
+        pltpu.VMEM((len(PAIRS) * ROWS, 128), BF16),
+        pltpu.VMEM((len(PAIRS) * ROWS, 128), BF16),
+        pltpu.VMEM((len(PAIRS) * ROWS, 128), BF16),
+        pltpu.VMEM((HEADS * ROWS, ROWS), BF16),
+        pltpu.VMEM((ROWS, HEADS * ROWS), BF16),
         pltpu.VMEM((ROWS, HW), BF16),
-        pltpu.VMEM((ROWS, 3 * HW), BF16),
+        pltpu.VMEM((ROWS, 2048), BF16),
         pltpu.VMEM((CHUNKS, ROWS, CW), F32),
         pltpu.VMEM((ROWS, 1), F32),
+        pltpu.VMEM((3 * HW, VD), BF16),
+        pltpu.VMEM((FR, 1, 3 * HW), F32),
+        pltpu.VMEM((FR, 1, HW), F32),
         pltpu.VMEM((VD, NM * ROWS), BF16),
         pltpu.VMEM((NM * ROWS, HW), BF16),
-        pltpu.VMEM((2048, ROWS), BF16),
         pltpu.VMEM((VD + 32, ROWS), F32),
         pltpu.VMEM((2048, ROWS), BF16),
-        pltpu.VMEM((256, NM * ROWS), BF16),
+        pltpu.VMEM((NM * ROWS, 256), BF16),
         pltpu.VMEM((256, NM * ROWS), BF16),
         pltpu.VMEM((1, 1, VD), F32),
         pltpu.VMEM((NM, 1, VD), F32),
-        pltpu.VMEM((1, 1, VD), F32),
+        pltpu.VMEM((2, 1, VD), F32),
         pltpu.VMEM((NZ, 1, VD), F32),
-        pltpu.VMEM((ZR, 256), F32),
+        pltpu.VMEM((ZR + 32, 256), F32),
         pltpu.VMEM((32, HW), F32),
         pltpu.VMEM((8, ZR, 256), BF16),
         pltpu.VMEM((8, 32, HW), BF16),
         pltpu.VMEM((8, ZR, 256), BF16),
         pltpu.VMEM((8, 32, HW), BF16),
-        pltpu.VMEM((NM, 24, 256), F32),
-        pltpu.VMEM((NM, 24, 256), F32),
-        dma((8,)), dma((CHUNKS,)), dma((2 * CHUNKS,)),
+        pltpu.VMEM((NM, 32, 256), BF16),
+        pltpu.VMEM((NM, 32, 256), BF16),
+        dma((8,)), dma((CHUNKS,)), dma((2 * CHUNKS + 3,)),
         dma((CHUNKS,)), dma((CHUNKS,)), dma((CHUNKS,)), dma((CHUNKS,)),
     ] + [dma((8,)) for _ in range(18)]
     shapes = (
@@ -581,7 +630,7 @@
         kernel,
         out_shape=shapes,
         in_specs=[hbm] * 6,
-        out_specs=(hbm, hbm, vmem, vmem, vmem),
+        out_specs=(hbm,) * 5,
         scratch_shapes=scratch,
         compiler_params=pltpu.CompilerParams(
             collective_id=0, has_side_effects=True, vmem_limit_bytes=60 * 1024 * 1024
@@ -590,9 +639,9 @@
     act, gin, out_q, out_o, own_gain = pl.pallas_call(
         finish,
         out_shape=shapes[:4] + (jax.ShapeDtypeStruct((1, FR), F32),),
-        in_specs=[hbm] * 4 + [vmem],
-        out_specs=(hbm,) * 4 + (vmem,),
-        scratch_shapes=[pltpu.VMEM(x.shape, x.dtype) for x in shapes[:4]] + [dma((8,))],
+        in_specs=[hbm] * 5,
+        out_specs=(hbm,) * 5,
+        scratch_shapes=[pltpu.VMEM(x.shape, x.dtype) for x in shapes] + [pltpu.VMEM((1, FR), F32), dma((10,))],
         compiler_params=pltpu.CompilerParams(vmem_limit_bytes=60 * 1024 * 1024),
     )(*results)
     return (

time: 106 us -> 98.4 us (0.928)
  Pallas kernels: 105 us -> 97.4 us
    pallas_call x1, Pallas kernels: 102 us -> 95.5 us  [on_device(): pl.pallas_call(kernel, out_shape=shapes, in_specs=[hbm] * 6, out_specs=(h...]
    pallas_call x1, Pallas kernels: 3.13 us -> 1.96 us  [on_device(): pl.pallas_call(finish, out_shape=shapes[:4] + (jax.ShapeDtypeStruct((1, F...]
where the time goes in v3:
time: 98.4 us; the launch traced here: 98.2 us
  Pallas kernels  97.4 us (99%)
    pallas_call x1, Pallas kernels, on_device(): pl.pallas_call(kernel, out_shape=shapes, in_specs=[hbm] * 6, out_specs=(h...  95.5 us

profile of v3, /device:TPU:1, one launch (start us, length us, event | category | flops | bytes accessed | tf_op | source)
XLA Modules:
  0.0 98.2 jit_solution(17930541649276358798)
XLA Ops:
  0.6 95.5 %shard_map.101 = (bf16[128,1280]{1,0:T(8,128)(2,1)}, bf16[128,1280]{1,0:T(8,128)(2,1)}, f32[20,1,1920]{2,1,0:T(1,128)}, f32[20,1,640]{2,1,0:T(1,128)}, f32[1,1280]{1,0:T(1,128)}) custom-call(bf16[128,1280]{1,0:T(8,128)(2,1)} %bitcast.10, bf16[128,1280]{1,0:T(8,128)(2,1)} %bitcast.11, s32[1,128]{1,0:T(1,128)} %win_hbm.1, f32[1,1280]{1,0:T(1,128)} %gain_hbm.1, ...), custom_call_target="tpu_custom_call" | custom-call | tf_op jit(solution)/shard_map/pallas_call | solution.py:629
  96.1 2.0 %shard_map.102 = (bf16[128,1280]{1,0:T(8,128)(2,1)}, bf16[128,1280]{1,0:T(8,128)(2,1)}, f32[20,1,1920]{2,1,0:T(1,128)}, f32[20,1,640]{2,1,0:T(1,128)}, f32[1,20]{1,0:T(1,128)}) custom-call(bf16[128,1280]{1,0:T(8,128)(2,1)} %get-tuple-element.15.act, bf16[128,1280]{1,0:T(8,128)(2,1)} %get-tuple-element.16.gin, f32[20,1,1920]{2,1,0:T(1,128)} %get-tuple-element.17.out_q, ...), custom_call_target="tpu_custom_call" | custom-call | tf_op jit(solution)/shard_map/pallas_call | solution.py:639

commit v4 on v3

--- a/solution.py
+++ b/solution.py
@@ -15,6 +15,9 @@
 NS = 4
 CHUNKS = 5
 CW = VD // CHUNKS
+FAR = CHUNKS - 1
+SENT = (FAR,) + tuple(range(FAR))
+HALF = ROWS // 2
 ZR = VD // NZ
 FR = ZR // NM
 SCALE = HEAD**-0.5
@@ -73,10 +76,10 @@
     patches, cot, win_hbm, gain_hbm, wq_hbm, wo_hbm,
     act, gin, out_q, out_o, out_gain,
     wq, wo, win, gain, hbuf, gbuf, hout, gout, pacc, dacc, packed, pt32, ptb, ptl, att, mk, qm, km, vm, dam, dsr, dsl,
-    datt, dp, lifted, rs, wqt, oq, oo,
-    ngt, atg, gt32, gperm, dpg, gpg, dgain, dgrecv, dgz, dgzrecv,
+    datt, dp, lifted, rs, wqt, oq, oo, rbuf,
+    ngt, atg, gt32, gp32, gperm, dpg, gpg, o32, opad, dgain, dgrecv, dgz, dgzrecv,
     rq, ro, sq, so, zq, zo, fin, finrecv,
-    w_sem, in_sem, o_sem, hs, hr, gs, gr, ns, nr, as_, ar, ds, dr, ps, pr, vs, vr, us, ur, qs, qr, os_, or_, fs, fr,
+    w_sem, in_sem, o_sem, hs, hr, gs, gr, ns, nr, as_, ar, ds, dr, ps, pr, vs, vr, us, ur, qs, qr, os_, or_, fs, fr, ls, lr, ts,
 ):
     s = lax.axis_index("section")
     m = lax.axis_index("mp")
@@ -120,7 +123,7 @@
         pl.semaphore_signal(barrier, inc=1, device_id={"mp": lax.rem(m + d, NM)}, device_id_type=MESH)
     for d in range(1, NZ):
         pl.semaphore_signal(barrier, inc=1, device_id={"dp": lax.rem(z + d, NZ)}, device_id_type=MESH)
-    for d in (1, NS - 1):
+    for d in range(1, NS):
         pl.semaphore_signal(barrier, inc=1, device_id={"section": lax.rem(s + d, NS)}, device_id_type=MESH)
 
     dp[:, 3 * HW : 2048] = jnp.zeros((ROWS, 2048 - 3 * HW), BF16)
@@ -129,7 +132,7 @@
         cols = lax.broadcasted_iota(jnp.int32, (ROWS, 128), 1) + t * 128
         inside = (cols >= HEAD * h) & (cols < HEAD * h + HEAD)
         mk[i] = jnp.where(inside, 1.0, 0.0).astype(BF16)
-    gt32[VD : VD + 32, :] = jnp.zeros((32, ROWS), F32)
+    o32[ZR : ZR + 16, :] = jnp.zeros((16, HW), F32)
 
     def remote(src, dst, ssem, rsem, where):
         return pltpu.make_async_remote_copy(
@@ -142,11 +145,129 @@
     def hop_back(j):
         return remote(gout.at[j], gbuf.at[j], gs.at[j], gr.at[j], {"section": lax.rem(s + NS - 1, NS)})
 
+    def half_rows(i):
+        return pl.ds(i * HALF, HALF)
+
+    def far_forward(i):
+        slot = lax.rem(s, 2)
+        to = {"section": lax.rem(s + 3 - lax.rem(s, 2), NS)}
+        return remote(hout.at[FAR, half_rows(i)], rbuf.at[slot, i], ls.at[i], lr.at[slot * 2 + i], to)
+
+    def far_back(i):
+        slot = 3 - lax.rem(s, 2)
+        to = {"section": lax.rem(s + 2 - lax.rem(s, 2), NS)}
+        return remote(gout.at[FAR, half_rows(i)], rbuf.at[slot, i], ls.at[2 + i], lr.at[slot * 2 + i], to)
+
+    def near_forward():
+        half = half_rows(1)
+        to = {"section": lax.rem(s + 1, NS)}
+        return remote(hout.at[FAR, half], hbuf.at[FAR, half], hs.at[FAR], hr.at[FAR + 1], to)
+
+    def near_back():
+        half = half_rows(1)
+        to = {"section": lax.rem(s + NS - 1, NS)}
+        return remote(gout.at[FAR, half], gbuf.at[FAR, half], gs.at[FAR], gr.at[FAR + 1], to)
+
+    def pass_on(slot, i):
+        to = {"section": lax.rem(s + (2, 3, 2, 1)[slot], NS)}
+        if slot < 2:
+            return remote(rbuf.at[slot, i], hbuf.at[FAR, half_rows(i)], ts.at[slot * 2 + i], hr.at[FAR + i], to)
+        return remote(rbuf.at[slot, i], gbuf.at[FAR, half_rows(i)], ts.at[slot * 2 + i], gr.at[FAR + i], to)
+
+    def relay(slot):
+        for i in range(1):
+            remote(rbuf.at[slot, i], rbuf.at[slot, i], ts.at[slot * 2 + i], lr.at[slot * 2 + i], {"section": lax.rem(s + 1, NS)}).wait_recv()
+            pass_on(slot, i).start()
+
+    def forward_send(j):
+        if j == FAR:
+            far_forward(0).start()
+        else:
+            hop_forward(j).start()
+            if j == FAR - 1:
+                near_forward().start()
+
+    def forward_arrived(j):
+        if j == FAR:
+            pass_on(0, 0).wait_recv()
+            near_forward().wait_recv()
+        else:
+            hop_forward(j).wait_recv()
+
+    def back_send(j):
+        if j == FAR:
+            far_back(0).start()
+        else:
+            hop_back(j).start()
+            if j == FAR - 1:
+                near_back().start()
+
+    def back_arrived(j):
+        if j == FAR:
+            pass_on(2, 0).wait_recv()
+            near_back().wait_recv()
+        else:
+            hop_back(j).wait_recv()
+
     def mp_lanes(i):
         return pl.ds(pl.multiple_of(i * ROWS, ROWS), ROWS)
 
     def fold(x):
         return x[:, 0:128] + x[:, 128:256]
+
+    def column_copy(half, d):
+        to = lax.rem(m + d, NM)
+        cols = pl.ds(pl.multiple_of(to * 256 + half * 128, 128), 128)
+        i = half * NM + d
+        return remote(dp.at[:, cols], dpg.at[half, mp_lanes(m), :], ds.at[i], dr.at[i], {"mp": to})
+
+    def g_copy(d):
+        to = lax.rem(m + d, NM)
+        rows = pl.ds(pl.multiple_of(to * ZR, 16), ZR)
+        return remote(gperm.at[rows], gpg.at[:, mp_lanes(m)], ps.at[d], pr.at[d], {"mp": to})
+
+    def columns_q():
+        for half in range(2):
+            for d in range(1, NM):
+                column_copy(half, d).start()
+        for half in range(2):
+            cols = pl.ds(pl.multiple_of(m * 256 + half * 128, 128), 128)
+            dpg[half, mp_lanes(m), :] = dp[:, cols]
+
+    def turn_g(j):
+        gt32[j * CW : (j + 1) * CW, :] = gbuf[j].astype(F32).T
+        for first in range(0, VD, FR):
+            if (first + FR - 1) // CW == j:
+                i, k = first // FR % NM, first // FR // NM
+                gp32[i * ZR + k * FR : i * ZR + k * FR + FR, :] = gt32[first : first + FR, :]
+
+    def columns_g():
+        gperm[...] = gp32[...].astype(BF16)
+        for d in range(1, NM):
+            g_copy(d).start()
+        gpg[:, mp_lanes(m)] = gperm[pl.ds(pl.multiple_of(m * ZR, 16), ZR), :]
+
+    def attend_back(j):
+        part = nt(gbuf[j], wo[:, j * CW : (j + 1) * CW])
+        if j == 0:
+            dacc[...] = part
+        else:
+            dacc[...] += part
+
+    @pl.when(s > 0)
+    def _():
+        load_wo.wait()
+        pl.semaphore_wait(barrier, (NM - 1) + (NZ - 1) + (NS - 1))
+
+    @pl.when(s == NS - 1)
+    def _():
+        for j in range(CHUNKS):
+            load_cot(j).wait()
+            attend_back(j)
+            turn_g(j)
+        columns_g()
+        relay(0)
+        relay(1)
 
     load_gain.wait()
     @pl.when(s >= 2)
@@ -164,7 +285,7 @@
 
         @pl.when(s > 0)
         def _():
-            hop_forward(j).wait_recv()
+            forward_arrived(j)
 
         @pl.when(s < 2)
         def _():
@@ -201,8 +322,11 @@
         ptb[h * ROWS : (h + 1) * ROWS, :] = p.astype(BF16)
     for t in range(HW // 128):
         att[:, t * 128 : t * 128 + 128] = tn(ptb[head_rows(t), :], vm[pair_rows(t), :]).astype(BF16)
-    load_wo.wait()
-    pl.semaphore_wait(barrier, (NM - 1) + (NZ - 1) + 2)
+
+    @pl.when(s == 0)
+    def _():
+        load_wo.wait()
+        pl.semaphore_wait(barrier, (NM - 1) + (NZ - 1) + (NS - 1))
 
     def project(j):
         hout[j] = (hbuf[j].astype(F32) + nn(att[...], wo[:, j * CW : (j + 1) * CW])).astype(BF16)
@@ -245,13 +369,13 @@
 
     @pl.when(s < NS - 1)
     def _():
-        for j in range(CHUNKS):
+        for j in SENT:
             project(j)
-            hop_forward(j).start()
+            forward_send(j)
 
     gather_start()
 
-    @pl.when(s < NS - 2)
+    @pl.when(s == 0)
     def _():
         gather_forward()
 
@@ -262,62 +386,34 @@
     @pl.when(s < 2)
     def _():
         turn_weights()
+
+    @pl.when(s == 1)
+    def _():
+        relay(0)
+        gather_forward()
+
+    @pl.when(s == 0)
+    def _():
+        relay(2)
+        relay(3)
 
     for i, (t, h) in enumerate(PAIRS):
         qm[i * ROWS : (i + 1) * ROWS, :] = packed[:, t * 128 : t * 128 + 128] * mk[i]
     for h in range(HEADS):
         ptl[:, h * ROWS : (h + 1) * ROWS] = ptb[h * ROWS : (h + 1) * ROWS, :]
 
-    def column_copy(which, d):
-        to = lax.rem(m + d, NM)
-        rows = pl.ds(pl.multiple_of(to * 256, 256), 256)
-        lanes = mp_lanes(m)
-        if which == 0:
-            return remote(dp.at[:, rows], dpg.at[lanes, :], ds.at[d], dr.at[d], {"mp": to})
-        return remote(gperm.at[rows], gpg.at[:, lanes], ps.at[d], pr.at[d], {"mp": to})
-
-    def columns_q():
-        for d in range(1, NM):
-            column_copy(0, d).start()
-        dpg[mp_lanes(m), :] = dp[:, pl.ds(pl.multiple_of(m * 256, 256), 256)]
-
-    def turn_g(j):
-        gt32[j * CW : (j + 1) * CW, :] = gbuf[j].astype(F32).T
-
-    def columns_g():
-        for i in range(NM):
-            for j in range(NZ):
-                first = FR * (NM * j + i)
-                gperm[i * 256 + j * 32 : i * 256 + j * 32 + 32, :] = gt32[first : first + 32, :].astype(BF16)
-        for d in range(1, NM):
-            column_copy(1, d).start()
-        gpg[:, mp_lanes(m)] = gperm[pl.ds(pl.multiple_of(m * 256, 256), 256), :]
-
     for j in range(CHUNKS):
-
-        @pl.when(s == NS - 1)
-        def _():
-            load_cot(j).wait()
 
         @pl.when(s < NS - 1)
         def _():
-            hop_back(j).wait_recv()
-
-        part = nt(gbuf[j], wo[:, j * CW : (j + 1) * CW])
-        if j == 0:
-            dacc[...] = part
-        else:
-            dacc[...] += part
+            back_arrived(j)
+            attend_back(j)
 
         @pl.when(s == 0)
         def _():
             turn_g(j)
 
     datt[...] = dacc[...].astype(BF16)
-
-    @pl.when(s == 0)
-    def _():
-        columns_g()
 
     for i, (t, h) in enumerate(PAIRS):
         dam[i * ROWS : (i + 1) * ROWS, :] = datt[:, t * 128 : t * 128 + 128] * mk[i]
@@ -340,24 +436,25 @@
     @pl.when(s == 0)
     def _():
         columns_q()
-
+        columns_g()
+
+    spread = rs[...]
     inner = jnp.zeros((ROWS, 128), F32)
-    for j in range(CHUNKS):
+    for t in range(3 * HW // 128):
+        cols = slice(t * 128, t * 128 + 128)
+        inner = inner + dp[:, cols].astype(F32) * pacc[:, cols]
+    pull = jnp.sum(inner, axis=-1, keepdims=True) * (1.0 / VD) * (spread * spread * spread)
+    for j in SENT:
         dn = nn(dp[:, 0 : 3 * HW], wqt[:, j * CW : (j + 1) * CW]).astype(BF16).astype(F32)
-        wide = hbuf[j].astype(F32)
         up = dn * gain[:, j * CW : (j + 1) * CW]
-        lifted[j] = up
-        inner = inner + fold(up * wide)
-        dgain[0, :, j * CW : (j + 1) * CW] = jnp.sum(dn * (wide * rs[...]), axis=0, keepdims=True)
-    spread = rs[...]
-    pull = jnp.sum(inner, axis=-1, keepdims=True) * (1.0 / VD) * (spread * spread * spread)
-    for j in range(CHUNKS):
-        back = gbuf[j].astype(F32) + spread * lifted[j] - hbuf[j].astype(F32) * pull
+        back = gbuf[j].astype(F32) + spread * up - hbuf[j].astype(F32) * pull
         gout[j] = back.astype(BF16)
 
         @pl.when(s > 0)
         def _():
-            hop_back(j).start()
+            back_send(j)
+
+        lifted[j] = dn
 
     def store_act(j):
         return pltpu.make_async_copy(hout.at[j], act.at[:, cols_of(j)], o_sem.at[j])
@@ -371,10 +468,17 @@
     @pl.when(s > 0)
     def _():
         columns_q()
+
+    @pl.when((s > 0) & (s < NS - 1))
+    def _():
         for j in range(CHUNKS):
             turn_g(j)
         columns_g()
 
+    for j in range(CHUNKS):
+        part = lifted[j] * (hbuf[j].astype(F32) * rs[...])
+        dgain[0, :, j * CW : (j + 1) * CW] = jnp.sum(part, axis=0, keepdims=True)
+
     @pl.when(s == NS - 1)
     def _():
         for j in range(CHUNKS):
@@ -384,6 +488,10 @@
     def _():
         gather_forward()
 
+    @pl.when(s == 2)
+    def _():
+        relay(2)
+
     for j in range(CHUNKS):
         store_act(j).start()
 
@@ -396,13 +504,15 @@
     for d in range(1, NM):
         gain_mp(d).start()
 
-    def chunk_q(k):
-        rows = pl.ds(pl.multiple_of(k * ZR, 16), ZR)
-        return nn(ngt[rows, :], dpg[...])
+    def chunk_q(half):
+        def chunk(k):
+            rows = pl.ds(pl.multiple_of(k * ZR, 16), ZR)
+            return nn(ngt[rows, :], dpg[half])
+
+        return chunk
 
     def chunk_o(k):
-        rows = pl.ds(pl.multiple_of(k * 32, 32), 32)
-        return nn(gpg[rows, :], atg[...])
+        return opad[k]
 
     steps = (NZ - 1, 1, NZ - 2, 2, NZ - 1, 1, NZ - 2, 2)
     owners = (NZ - 3, 3, 4, 4, NZ - 1, 1, NZ - 2, 2)
@@ -410,11 +520,15 @@
     def peer(i):
         return {"dp": lax.rem(z + steps[i], NZ)}
 
-    def tree_q(i):
-        if i == 2 or i == 3:
-            half = pl.ds(0, ZR // 2)
-            return remote(sq.at[i, half], zq.at[i, half], qs.at[i], qr.at[i], peer(i))
-        return remote(sq.at[i], zq.at[i], qs.at[i], qr.at[i], peer(i))
+    def tree_q(half):
+        def copy(i):
+            n = half * 8 + i
+            if i == 2 or i == 3:
+                top = pl.ds(0, ZR // 2)
+                return remote(sq.at[half, i, top], zq.at[half, i, top], qs.at[n], qr.at[n], peer(i))
+            return remote(sq.at[half, i], zq.at[half, i], qs.at[n], qr.at[n], peer(i))
+
+        return copy
 
     def tree_o(i):
         if i == 2 or i == 3:
@@ -448,25 +562,42 @@
         buf[i] = hold[...].astype(BF16)
         copy(i).start()
 
+    def leaf_q(half, i):
+        leaf(i, chunk_q(half), sq.at[half], tree_q(half), ZR)
+
+    def sum_of(half):
+        return rq.at[0:ZR, half * 128 : half * 128 + 128]
+
+    def branch_q(half, i):
+        branch(i, chunk_q(half), sq.at[half], zq.at[half], tree_q(half), ZR, sum_of(half))
+
+    gather_finish(0)
+    for half in range(2):
+        for d in range(1, NM):
+            column_copy(half, d).wait_recv()
+        for i in (2, 0, 1):
+            leaf_q(half, i)
+    for i in (4, 5):
+        leaf_q(0, i)
+    for i in (6, 7):
+        branch_q(0, i)
+
     gather_finish(1)
     for d in range(1, NM):
-        column_copy(1, d).wait_recv()
-    for i in (2, 0, 1, 4, 5):
+        g_copy(d).wait_recv()
+    o32[0:ZR, :] = nn(gpg[...], atg[...])
+    for k in range(NZ):
+        opad[k] = o32[FR * k : FR * k + 32, :]
+    for i in (2, 0, 1):
         leaf(i, chunk_o, so, tree_o, 32)
-
-    gather_finish(0)
-    for d in range(1, NM):
-        column_copy(0, d).wait_recv()
-    for i in (2, 0, 1):
-        leaf(i, chunk_q, sq, tree_q, ZR)
-
+    for i in (4, 5):
+        leaf_q(1, i)
+    for i in (6, 7):
+        branch_q(1, i)
+    for i in (4, 5):
+        leaf(i, chunk_o, so, tree_o, 32)
     for i in (6, 7):
         branch(i, chunk_o, so, zo, tree_o, 32, ro)
-    for i in (4, 5):
-        leaf(i, chunk_q, sq, tree_q, ZR)
-
-    for i in (6, 7):
-        branch(i, chunk_q, sq, zq, tree_q, ZR, rq.at[0:ZR])
 
     sum_gain = dgain[0]
     for d in range(1, NM):
@@ -476,6 +607,22 @@
     for d in range(1, NZ):
         gain_dp(d).start()
 
+    for half in range(2):
+        hold = sum_of(half)
+        hold[...] = chunk_q(half)(z)
+        for i in (4, 5, 6, 7):
+            tree_q(half)(i).wait_recv()
+            hold[...] += zq[half, i].astype(F32)
+
+    def piece(d):
+        return remote(fin.at[lax.rem(m + d, NM)], finrecv.at[m], fs.at[d], fr.at[d], {"mp": lax.rem(m + d, NM)})
+
+    for i in range(NM):
+        fin[i] = rq[FR * i : FR * i + 32, :].astype(BF16)
+    for d in range(1, NM):
+        piece(d).start()
+    finrecv[m] = fin[m]
+
     ro[...] = chunk_o(z)
     for i in (4, 5, 6, 7):
         tree_o(i).wait_recv()
@@ -484,20 +631,6 @@
     store_o = pltpu.make_async_copy(oo, out_o, o_sem.at[2 * CHUNKS])
     store_o.start()
 
-    rq[0:ZR, :] = chunk_q(z)
-    for i in (4, 5, 6, 7):
-        tree_q(i).wait_recv()
-        rq[0:ZR, :] += zq[i].astype(F32)
-
-    def piece(d):
-        return remote(fin.at[lax.rem(m + d, NM)], finrecv.at[m], fs.at[d], fr.at[d], {"mp": lax.rem(m + d, NM)})
-
-    for i in range(NM):
-        fin[i] = rq[FR * i : FR * i + 32, :].astype(BF16)
-    for d in range(1, NM):
-        piece(d).start()
-    finrecv[m] = fin[m]
-
     sum_gain = dgz[0]
     for d in range(1, NZ):
         gain_dp(d).wait_recv()
@@ -508,25 +641,38 @@
 
     @pl.when(s < NS - 1)
     def _():
-        for j in range(CHUNKS):
+        for j in range(FAR):
             hop_forward(j).wait_send()
+        far_forward(0).wait_send()
+        near_forward().wait_send()
 
     @pl.when(s > 0)
     def _():
-        for j in range(CHUNKS):
+        for j in range(FAR):
             hop_back(j).wait_send()
+        far_back(0).wait_send()
+        near_back().wait_send()
+
+    for where, slots in ((0, (2, 3)), (1, (0,)), (2, (2,)), (3, (0, 1))):
+
+        @pl.when(s == where)
+        def _():
+            for slot in slots:
+                pass_on(slot, 0).wait_send()
 
     for i in range(NM - 1):
         for w in range(2):
             gather_copy(w, m, i, sibling).wait_send()
     for d in range(1, NM):
-        for w in range(2):
-            column_copy(w, d).wait_send()
+        for half in range(2):
+            column_copy(half, d).wait_send()
+        g_copy(d).wait_send()
         gain_mp(d).wait_send()
     for d in range(1, NZ):
         gain_dp(d).wait_send()
     for i in range(8):
-        tree_q(i).wait_send()
+        tree_q(0)(i).wait_send()
+        tree_q(1)(i).wait_send()
         tree_o(i).wait_send()
     for j in range(CHUNKS):
         store_act(j).wait()
@@ -598,27 +744,31 @@
         pltpu.VMEM((3 * HW, VD), BF16),
         pltpu.VMEM((FR, 1, 3 * HW), F32),
         pltpu.VMEM((FR, 1, HW), F32),
+        pltpu.VMEM((4, 2, HALF, CW), BF16),
         pltpu.VMEM((VD, NM * ROWS), BF16),
         pltpu.VMEM((NM * ROWS, HW), BF16),
-        pltpu.VMEM((VD + 32, ROWS), F32),
-        pltpu.VMEM((2048, ROWS), BF16),
-        pltpu.VMEM((NM * ROWS, 256), BF16),
-        pltpu.VMEM((256, NM * ROWS), BF16),
+        pltpu.VMEM((VD, ROWS), F32),
+        pltpu.VMEM((VD, ROWS), F32),
+        pltpu.VMEM((VD, ROWS), BF16),
+        pltpu.VMEM((2, NM * ROWS, 128), BF16),
+        pltpu.VMEM((ZR, NM * ROWS), BF16),
+        pltpu.VMEM((ZR + 16, HW), F32),
+        pltpu.VMEM((NZ, 32, HW), F32),
         pltpu.VMEM((1, 1, VD), F32),
         pltpu.VMEM((NM, 1, VD), F32),
         pltpu.VMEM((2, 1, VD), F32),
         pltpu.VMEM((NZ, 1, VD), F32),
         pltpu.VMEM((ZR + 32, 256), F32),
         pltpu.VMEM((32, HW), F32),
-        pltpu.VMEM((8, ZR, 256), BF16),
+        pltpu.VMEM((2, 8, ZR, 128), BF16),
         pltpu.VMEM((8, 32, HW), BF16),
-        pltpu.VMEM((8, ZR, 256), BF16),
+        pltpu.VMEM((2, 8, ZR, 128), BF16),
         pltpu.VMEM((8, 32, HW), BF16),
         pltpu.VMEM((NM, 32, 256), BF16),
         pltpu.VMEM((NM, 32, 256), BF16),
         dma((8,)), dma((CHUNKS,)), dma((2 * CHUNKS + 3,)),
-        dma((CHUNKS,)), dma((CHUNKS,)), dma((CHUNKS,)), dma((CHUNKS,)),
-    ] + [dma((8,)) for _ in range(18)]
+        dma((8,)), dma((8,)), dma((8,)), dma((8,)),
+    ] + [dma((16,)) for _ in range(21)]
     shapes = (
         jax.ShapeDtypeStruct((ROWS, VD), BF16),
         jax.ShapeDtypeStruct((ROWS, VD), BF16),

time: 98.4 us -> 93.2 us (0.947)
  Pallas kernels: 97.4 us -> 92.2 us
    pallas_call x1, Pallas kernels: 95.5 us -> 90.3 us  [on_device(): pl.pallas_call(kernel, out_shape=shapes, in_specs=[hbm] * 6, out_specs=(h...]
where the time goes in v4:
time: 93.2 us; the launch traced here: 93 us
  Pallas kernels  92.2 us (99%)
    pallas_call x1, Pallas kernels, on_device(): pl.pallas_call(kernel, out_shape=shapes, in_specs=[hbm] * 6, out_specs=(h...  90.3 us
    pallas_call x1, Pallas kernels, on_device(): pl.pallas_call(finish, out_shape=shapes[:4] + (jax.ShapeDtypeStruct((1, F...  1.96 us

profile of v4, /device:TPU:1, one launch (start us, length us, event | category | flops | bytes accessed | tf_op | source)
XLA Modules:
  0.0 93.0 jit_solution(10948156378880589171)
XLA Ops:
  0.6 90.3 %shard_map.101 = (bf16[128,1280]{1,0:T(8,128)(2,1)}, bf16[128,1280]{1,0:T(8,128)(2,1)}, f32[20,1,1920]{2,1,0:T(1,128)}, f32[20,1,640]{2,1,0:T(1,128)}, f32[1,1280]{1,0:T(1,128)}) custom-call(bf16[128,1280]{1,0:T(8,128)(2,1)} %bitcast.10, bf16[128,1280]{1,0:T(8,128)(2,1)} %bitcast.11, s32[1,128]{1,0:T(1,128)} %win_hbm.1, f32[1,1280]{1,0:T(1,128)} %gain_hbm.1, ...), custom_call_target="tpu_custom_call" | custom-call | tf_op jit(solution)/shard_map/pallas_call | solution.py:779
  90.9 2.0 %shard_map.102 = (bf16[128,1280]{1,0:T(8,128)(2,1)}, bf16[128,1280]{1,0:T(8,128)(2,1)}, f32[20,1,1920]{2,1,0:T(1,128)}, f32[20,1,640]{2,1,0:T(1,128)}, f32[1,20]{1,0:T(1,128)}) custom-call(bf16[128,1280]{1,0:T(8,128)(2,1)} %get-tuple-element.15.act, bf16[128,1280]{1,0:T(8,128)(2,1)} %get-tuple-element.16.gin, f32[20,1,1920]{2,1,0:T(1,128)} %get-tuple-element.17.out_q, ...), custom_call_target="tpu_custom_call" | custom-call | tf_op jit(solution)/shard_map/pallas_call | solution.py:789

commit v5 on v4

--- a/solution.py
+++ b/solution.py
@@ -132,7 +132,7 @@
         cols = lax.broadcasted_iota(jnp.int32, (ROWS, 128), 1) + t * 128
         inside = (cols >= HEAD * h) & (cols < HEAD * h + HEAD)
         mk[i] = jnp.where(inside, 1.0, 0.0).astype(BF16)
-    o32[ZR : ZR + 16, :] = jnp.zeros((16, HW), F32)
+    opad[:, :, HW : HW + 256] = jnp.zeros((NZ, 16, 256), F32)
 
     def remote(src, dst, ssem, rsem, where):
         return pltpu.make_async_remote_copy(
@@ -531,45 +531,54 @@
         return copy
 
     def tree_o(i):
-        if i == 2 or i == 3:
-            half = pl.ds(0, 16)
-            return remote(so.at[i, half], zo.at[i, half], os_.at[i], or_.at[i], peer(i))
-        return remote(so.at[i], zo.at[i], os_.at[i], or_.at[i], peer(i))
+        to = {"dp": lax.rem(z + NZ - 2 + 4 * core, NZ)} if i == 2 else peer(i)
+        return remote(so.at[i], zo.at[i], os_.at[i], or_.at[i], to)
 
     def whose(i):
         return lax.rem(z + owners[i], NZ)
 
-    def leaf(i, chunk, buf, copy, rows):
+    def leaf_o(i):
+        so[i] = chunk_o(whose(i)).astype(BF16)
+        tree_o(i).start()
+
+    def branch_o(i):
+        ro[...] = chunk_o(whose(i))
+        tree_o(i - 6).wait_recv()
+        ro[...] += zo[i - 6].astype(F32)
+
+        @pl.when(core == i - 6)
+        def _():
+            tree_o(2).wait_recv()
+            ro[...] += zo[2].astype(F32)
+
+        so[i] = ro[...].astype(BF16)
+        tree_o(i).start()
+
+    def leaf_q(half, i):
+        copy, buf = tree_q(half), sq.at[half]
         if i == 2:
-            value = chunk(whose(2)).astype(BF16)
-            buf[2, 0 : rows // 2] = value[0 : rows // 2]
-            buf[3, 0 : rows // 2] = value[rows // 2 : rows]
+            value = chunk_q(half)(whose(2)).astype(BF16)
+            buf[2, 0 : ZR // 2] = value[0 : ZR // 2]
+            buf[3, 0 : ZR // 2] = value[ZR // 2 : ZR]
             copy(2).start()
             copy(3).start()
         else:
-            buf[i] = chunk(whose(i)).astype(BF16)
+            buf[i] = chunk_q(half)(whose(i)).astype(BF16)
             copy(i).start()
-
-    def branch(i, chunk, buf, got, copy, rows, hold):
-        hold[...] = chunk(whose(i))
-        copy(i - 6).wait_recv()
-        hold[...] += got[i - 6].astype(F32)
-        copy(i - 4).wait_recv()
-        if i == 6:
-            hold[0 : rows // 2] += got[2, 0 : rows // 2].astype(F32)
-        else:
-            hold[rows // 2 : rows] += got[3, 0 : rows // 2].astype(F32)
-        buf[i] = hold[...].astype(BF16)
-        copy(i).start()
-
-    def leaf_q(half, i):
-        leaf(i, chunk_q(half), sq.at[half], tree_q(half), ZR)
 
     def sum_of(half):
         return rq.at[0:ZR, half * 128 : half * 128 + 128]
 
     def branch_q(half, i):
-        branch(i, chunk_q(half), sq.at[half], zq.at[half], tree_q(half), ZR, sum_of(half))
+        hold, copy = sum_of(half), tree_q(half)
+        hold[...] = chunk_q(half)(whose(i))
+        copy(i - 6).wait_recv()
+        hold[...] += zq[half, i - 6].astype(F32)
+        copy(i - 4).wait_recv()
+        top = 0 if i == 6 else ZR // 2
+        hold[top : top + ZR // 2] += zq[half, i - 4, 0 : ZR // 2].astype(F32)
+        sq[half, i] = hold[...].astype(BF16)
+        copy(i).start()
 
     gather_finish(0)
     for half in range(2):
@@ -587,17 +596,37 @@
         g_copy(d).wait_recv()
     o32[0:ZR, :] = nn(gpg[...], atg[...])
     for k in range(NZ):
-        opad[k] = o32[FR * k : FR * k + 32, :]
+        opad[k, :, 0:HW] = o32[FR * k : FR * k + 16, :]
+        for t in range(HW // 128):
+            row, col = 4 * (t % 4), HW + t // 4 * 128
+            opad[k, row : row + 4, col : col + 128] = o32[FR * k + 16 : FR * k + FR, t * 128 : t * 128 + 128]
     for i in (2, 0, 1):
-        leaf(i, chunk_o, so, tree_o, 32)
+        leaf_o(i)
     for i in (4, 5):
         leaf_q(1, i)
     for i in (6, 7):
         branch_q(1, i)
     for i in (4, 5):
-        leaf(i, chunk_o, so, tree_o, 32)
+        leaf_o(i)
     for i in (6, 7):
-        branch(i, chunk_o, so, zo, tree_o, 32, ro)
+        branch_o(i)
+
+    def piece(half, to, slot, d):
+        i = half * NM + d
+        return remote(fin.at[half, to], finrecv.at[half, slot], fs.at[i], fr.at[i], {"mp": to})
+
+    for half in range(2):
+        hold = sum_of(half)
+        hold[...] = chunk_q(half)(z)
+        for i in (4, 5, 6, 7):
+            tree_q(half)(i).wait_recv()
+            hold[...] += zq[half, i].astype(F32)
+        cols = slice(half * 128, half * 128 + 128)
+        for i in range(NM):
+            fin[half, i] = rq[FR * i : FR * i + 32, cols].astype(BF16)
+        for d in range(1, NM):
+            piece(half, lax.rem(m + d, NM), m, d).start()
+        finrecv[half, m] = fin[half, m]
 
     sum_gain = dgain[0]
     for d in range(1, NM):
@@ -607,27 +636,14 @@
     for d in range(1, NZ):
         gain_dp(d).start()
 
-    for half in range(2):
-        hold = sum_of(half)
-        hold[...] = chunk_q(half)(z)
-        for i in (4, 5, 6, 7):
-            tree_q(half)(i).wait_recv()
-            hold[...] += zq[half, i].astype(F32)
-
-    def piece(d):
-        return remote(fin.at[lax.rem(m + d, NM)], finrecv.at[m], fs.at[d], fr.at[d], {"mp": lax.rem(m + d, NM)})
-
-    for i in range(NM):
-        fin[i] = rq[FR * i : FR * i + 32, :].astype(BF16)
-    for d in range(1, NM):
-        piece(d).start()
-    finrecv[m] = fin[m]
-
     ro[...] = chunk_o(z)
     for i in (4, 5, 6, 7):
         tree_o(i).wait_recv()
         ro[...] += zo[i].astype(F32)
-    oo[:, 0, :] = ro[0:FR, :]
+    oo[0:16, 0, :] = ro[:, 0:HW]
+    for t in range(HW // 128):
+        row, col = 4 * (t % 4), HW + t // 4 * 128
+        oo[16:FR, 0, t * 128 : t * 128 + 128] = ro[row : row + 4, col : col + 128]
     store_o = pltpu.make_async_copy(oo, out_o, o_sem.at[2 * CHUNKS])
     store_o.start()
 
@@ -673,21 +689,25 @@
     for i in range(8):
         tree_q(0)(i).wait_send()
         tree_q(1)(i).wait_send()
-        tree_o(i).wait_send()
+        if i != 3:
+            tree_o(i).wait_send()
     for j in range(CHUNKS):
         store_act(j).wait()
         store_gin(j).wait()
 
-    for d in range(1, NM):
-        source = lax.rem(m + NM - d, NM)
-        remote(fin.at[source], finrecv.at[source], fs.at[d], fr.at[d], {"mp": source}).wait_recv()
-    for i in range(NM):
-        wide = min(256, 3 * HW - 256 * i)
-        oq[:, 0, 256 * i : 256 * i + wide] = finrecv[i, :, 0:wide].astype(F32)[0:FR]
+    for half in range(2):
+        for d in range(1, NM):
+            source = lax.rem(m + NM - d, NM)
+            piece(half, source, source, d).wait_recv()
+        for i in range(NM):
+            first = 256 * i + 128 * half
+            if first < 3 * HW:
+                oq[:, 0, first : first + 128] = finrecv[half, i].astype(F32)[0:FR]
     store_q = pltpu.make_async_copy(oq, out_q, o_sem.at[2 * CHUNKS + 2])
     store_q.start()
-    for d in range(1, NM):
-        piece(d).wait_send()
+    for half in range(2):
+        for d in range(1, NM):
+            piece(half, lax.rem(m + d, NM), m, d).wait_send()
     store_o.wait()
     store_gain.wait()
     store_q.wait()
@@ -752,20 +772,20 @@
         pltpu.VMEM((VD, ROWS), BF16),
         pltpu.VMEM((2, NM * ROWS, 128), BF16),
         pltpu.VMEM((ZR, NM * ROWS), BF16),
-        pltpu.VMEM((ZR + 16, HW), F32),
-        pltpu.VMEM((NZ, 32, HW), F32),
+        pltpu.VMEM((ZR, HW), F32),
+        pltpu.VMEM((NZ, 16, HW + 256), F32),
         pltpu.VMEM((1, 1, VD), F32),
         pltpu.VMEM((NM, 1, VD), F32),
         pltpu.VMEM((2, 1, VD), F32),
         pltpu.VMEM((NZ, 1, VD), F32),
         pltpu.VMEM((ZR + 32, 256), F32),
-        pltpu.VMEM((32, HW), F32),
+        pltpu.VMEM((16, HW + 256), F32),
         pltpu.VMEM((2, 8, ZR, 128), BF16),
-        pltpu.VMEM((8, 32, HW), BF16),
+        pltpu.VMEM((8, 16, HW + 256), BF16),
         pltpu.VMEM((2, 8, ZR, 128), BF16),
-        pltpu.VMEM((8, 32, HW), BF16),
-        pltpu.VMEM((NM, 32, 256), BF16),
-        pltpu.VMEM((NM, 32, 256), BF16),
+        pltpu.VMEM((8, 16, HW + 256), BF16),
+        pltpu.VMEM((2, NM, 32, 128), BF16),
+        pltpu.VMEM((2, NM, 32, 128), BF16),
         dma((8,)), dma((CHUNKS,)), dma((2 * CHUNKS + 3,)),
         dma((8,)), dma((8,)), dma((8,)), dma((8,)),
     ] + [dma((16,)) for _ in range(21)]

time: 93.2 us -> 91.9 us (0.986)
  Pallas kernels: 92.2 us -> 90.5 us
    pallas_call x1, Pallas kernels: 90.3 us -> 88.6 us  [on_device(): pl.pallas_call(kernel, out_shape=shapes, in_specs=[hbm] * 6, out_specs=(h...]
where the time goes in v5:
time: 91.9 us; the launch traced here: 91.3 us
  Pallas kernels  90.5 us (98%)
    pallas_call x1, Pallas kernels, on_device(): pl.pallas_call(kernel, out_shape=shapes, in_specs=[hbm] * 6, out_specs=(h...  88.6 us
    pallas_call x1, Pallas kernels, on_device(): pl.pallas_call(finish, out_shape=shapes[:4] + (jax.ShapeDtypeStruct((1, F...  1.96 us

profile of v5, /device:TPU:1, one launch (start us, length us, event | category | flops | bytes accessed | tf_op | source)
XLA Modules:
  0.0 91.3 jit_solution(14893073689282890426)
XLA Ops:
  0.6 88.6 %shard_map.101 = (bf16[128,1280]{1,0:T(8,128)(2,1)}, bf16[128,1280]{1,0:T(8,128)(2,1)}, f32[20,1,1920]{2,1,0:T(1,128)}, f32[20,1,640]{2,1,0:T(1,128)}, f32[1,1280]{1,0:T(1,128)}) custom-call(bf16[128,1280]{1,0:T(8,128)(2,1)} %bitcast.10, bf16[128,1280]{1,0:T(8,128)(2,1)} %bitcast.11, s32[1,128]{1,0:T(1,128)} %win_hbm.1, f32[1,1280]{1,0:T(1,128)} %gain_hbm.1, ...), custom_call_target="tpu_custom_call" | custom-call | tf_op jit(solution)/shard_map/pallas_call | solution.py:799
  89.2 2.0 %shard_map.102 = (bf16[128,1280]{1,0:T(8,128)(2,1)}, bf16[128,1280]{1,0:T(8,128)(2,1)}, f32[20,1,1920]{2,1,0:T(1,128)}, f32[20,1,640]{2,1,0:T(1,128)}, f32[1,20]{1,0:T(1,128)}) custom-call(bf16[128,1280]{1,0:T(8,128)(2,1)} %get-tuple-element.15.act, bf16[128,1280]{1,0:T(8,128)(2,1)} %get-tuple-element.16.gin, f32[20,1,1920]{2,1,0:T(1,128)} %get-tuple-element.17.out_q, ...), custom_call_target="tpu_custom_call" | custom-call | tf_op jit(solution)/shard_map/pallas_call | solution.py:809

commit v6 on v5

--- a/solution.py
+++ b/solution.py
@@ -168,6 +168,10 @@
         to = {"section": lax.rem(s + NS - 1, NS)}
         return remote(gout.at[FAR, half], gbuf.at[FAR, half], gs.at[FAR], gr.at[FAR + 1], to)
 
+    def last_back():
+        half = half_rows(0)
+        return remote(gout.at[FAR, half], gbuf.at[FAR, half], ls.at[2], gr.at[FAR], {"section": lax.rem(s + NS - 1, NS)})
+
     def pass_on(slot, i):
         to = {"section": lax.rem(s + (2, 3, 2, 1)[slot], NS)}
         if slot < 2:
@@ -196,7 +200,14 @@
 
     def back_send(j):
         if j == FAR:
-            far_back(0).start()
+
+            @pl.when(s > 1)
+            def _():
+                far_back(0).start()
+
+            @pl.when(s == 1)
+            def _():
+                last_back().start()
         else:
             hop_back(j).start()
             if j == FAR - 1:
@@ -409,9 +420,11 @@
             back_arrived(j)
             attend_back(j)
 
-        @pl.when(s == 0)
-        def _():
-            turn_g(j)
+        if j != FAR:
+
+            @pl.when(s == 0)
+            def _():
+                turn_g(j)
 
     datt[...] = dacc[...].astype(BF16)
 
@@ -436,6 +449,7 @@
     @pl.when(s == 0)
     def _():
         columns_q()
+        turn_g(FAR)
         columns_g()
 
     spread = rs[...]
@@ -487,10 +501,6 @@
     @pl.when(s >= NS - 2)
     def _():
         gather_forward()
-
-    @pl.when(s == 2)
-    def _():
-        relay(2)
 
     for j in range(CHUNKS):
         store_act(j).start()
@@ -666,10 +676,10 @@
     def _():
         for j in range(FAR):
             hop_back(j).wait_send()
-        far_back(0).wait_send()
+        last_back().wait_send()
         near_back().wait_send()
 
-    for where, slots in ((0, (2, 3)), (1, (0,)), (2, (2,)), (3, (0, 1))):
+    for where, slots in ((0, (2, 3)), (1, (0,)), (3, (0, 1))):
 
         @pl.when(s == where)
         def _():

time: 91.9 us -> 91.1 us (level)
  no operation moved by 1% of the time
where the time goes in v6:
time: 91.1 us; the launch traced here: 90.5 us
  Pallas kernels  89.7 us (98%)
    pallas_call x1, Pallas kernels, on_device(): pl.pallas_call(kernel, out_shape=shapes, in_specs=[hbm] * 6, out_specs=(h...  87.8 us
    pallas_call x1, Pallas kernels, on_device(): pl.pallas_call(finish, out_shape=shapes[:4] + (jax.ShapeDtypeStruct((1, F...  1.96 us

profile of v6, /device:TPU:1, one launch (start us, length us, event | category | flops | bytes accessed | tf_op | source)
XLA Modules:
  0.0 90.5 jit_solution(600364115986119065)
XLA Ops:
  0.6 87.8 %shard_map.101 = (bf16[128,1280]{1,0:T(8,128)(2,1)}, bf16[128,1280]{1,0:T(8,128)(2,1)}, f32[20,1,1920]{2,1,0:T(1,128)}, f32[20,1,640]{2,1,0:T(1,128)}, f32[1,1280]{1,0:T(1,128)}) custom-call(bf16[128,1280]{1,0:T(8,128)(2,1)} %bitcast.10, bf16[128,1280]{1,0:T(8,128)(2,1)} %bitcast.11, s32[1,128]{1,0:T(1,128)} %win_hbm.1, f32[1,1280]{1,0:T(1,128)} %gain_hbm.1, ...), custom_call_target="tpu_custom_call" | custom-call | tf_op jit(solution)/shard_map/pallas_call | solution.py:809
  88.4 2.0 %shard_map.102 = (bf16[128,1280]{1,0:T(8,128)(2,1)}, bf16[128,1280]{1,0:T(8,128)(2,1)}, f32[20,1,1920]{2,1,0:T(1,128)}, f32[20,1,640]{2,1,0:T(1,128)}, f32[1,20]{1,0:T(1,128)}) custom-call(bf16[128,1280]{1,0:T(8,128)(2,1)} %get-tuple-element.15.act, bf16[128,1280]{1,0:T(8,128)(2,1)} %get-tuple-element.16.gin, f32[20,1,1920]{2,1,0:T(1,128)} %get-tuple-element.17.out_q, ...), custom_call_target="tpu_custom_call" | custom-call | tf_op jit(solution)/shard_map/pallas_call | solution.py:819

commit v7 on v6

--- a/solution.py
+++ b/solution.py
@@ -618,16 +618,12 @@
         branch_q(1, i)
     for i in (4, 5):
         leaf_o(i)
-    for i in (6, 7):
-        branch_o(i)
-
     def piece(half, to, slot, d):
         i = half * NM + d
         return remote(fin.at[half, to], finrecv.at[half, slot], fs.at[i], fr.at[i], {"mp": to})
 
-    for half in range(2):
+    def settle(half):
         hold = sum_of(half)
-        hold[...] = chunk_q(half)(z)
         for i in (4, 5, 6, 7):
             tree_q(half)(i).wait_recv()
             hold[...] += zq[half, i].astype(F32)
@@ -637,6 +633,13 @@
         for d in range(1, NM):
             piece(half, lax.rem(m + d, NM), m, d).start()
         finrecv[half, m] = fin[half, m]
+
+    for half in range(2):
+        sum_of(half)[...] = chunk_q(half)(z)
+    settle(0)
+    for i in (6, 7):
+        branch_o(i)
+    settle(1)
 
     sum_gain = dgain[0]
     for d in range(1, NM):

time: 91.1 us -> 91.1 us (level)
  no operation moved by 1% of the time
where the time goes in v7:
time: 91.1 us; the launch traced here: 90.5 us
  Pallas kernels  89.7 us (98%)
    pallas_call x1, Pallas kernels, on_device(): pl.pallas_call(kernel, out_shape=shapes, in_specs=[hbm] * 6, out_specs=(h...  87.8 us
    pallas_call x1, Pallas kernels, on_device(): pl.pallas_call(finish, out_shape=shapes[:4] + (jax.ShapeDtypeStruct((1, F...  1.96 us

profile of v7, /device:TPU:1, one launch (start us, length us, event | category | flops | bytes accessed | tf_op | source)
XLA Modules:
  0.0 90.5 jit_solution(6961937705878680510)
XLA Ops:
  0.6 87.8 %shard_map.101 = (bf16[128,1280]{1,0:T(8,128)(2,1)}, bf16[128,1280]{1,0:T(8,128)(2,1)}, f32[20,1,1920]{2,1,0:T(1,128)}, f32[20,1,640]{2,1,0:T(1,128)}, f32[1,1280]{1,0:T(1,128)}) custom-call(bf16[128,1280]{1,0:T(8,128)(2,1)} %bitcast.10, bf16[128,1280]{1,0:T(8,128)(2,1)} %bitcast.11, s32[1,128]{1,0:T(1,128)} %win_hbm.1, f32[1,1280]{1,0:T(1,128)} %gain_hbm.1, ...), custom_call_target="tpu_custom_call" | custom-call | tf_op jit(solution)/shard_map/pallas_call | solution.py:812
  88.4 2.0 %shard_map.102 = (bf16[128,1280]{1,0:T(8,128)(2,1)}, bf16[128,1280]{1,0:T(8,128)(2,1)}, f32[20,1,1920]{2,1,0:T(1,128)}, f32[20,1,640]{2,1,0:T(1,128)}, f32[1,20]{1,0:T(1,128)}) custom-call(bf16[128,1280]{1,0:T(8,128)(2,1)} %get-tuple-element.15.act, bf16[128,1280]{1,0:T(8,128)(2,1)} %get-tuple-element.16.gin, f32[20,1,1920]{2,1,0:T(1,128)} %get-tuple-element.17.out_q, ...), custom_call_target="tpu_custom_call" | custom-call | tf_op jit(solution)/shard_map/pallas_call | solution.py:822

commit v8 on v6

--- a/solution.py
+++ b/solution.py
@@ -600,6 +600,8 @@
         leaf_q(0, i)
     for i in (6, 7):
         branch_q(0, i)
+    for i in (4, 5):
+        leaf_q(1, i)
 
     gather_finish(1)
     for d in range(1, NM):
@@ -612,8 +614,6 @@
             opad[k, row : row + 4, col : col + 128] = o32[FR * k + 16 : FR * k + FR, t * 128 : t * 128 + 128]
     for i in (2, 0, 1):
         leaf_o(i)
-    for i in (4, 5):
-        leaf_q(1, i)
     for i in (6, 7):
         branch_q(1, i)
     for i in (4, 5):

time: 91.1 us -> 90.7 us (level)
  no operation moved by 1% of the time
where the time goes in v8:
time: 90.7 us; the launch traced here: 90.4 us
  Pallas kernels  89.6 us (99%)
    pallas_call x1, Pallas kernels, on_device(): pl.pallas_call(kernel, out_shape=shapes, in_specs=[hbm] * 6, out_specs=(h...  87.6 us
    pallas_call x1, Pallas kernels, on_device(): pl.pallas_call(finish, out_shape=shapes[:4] + (jax.ShapeDtypeStruct((1, F...  1.96 us

profile of v8, /device:TPU:1, one launch (start us, length us, event | category | flops | bytes accessed | tf_op | source)
XLA Modules:
  0.0 90.4 jit_solution(14288708414075506826)
XLA Ops:
  0.6 87.6 %shard_map.101 = (bf16[128,1280]{1,0:T(8,128)(2,1)}, bf16[128,1280]{1,0:T(8,128)(2,1)}, f32[20,1,1920]{2,1,0:T(1,128)}, f32[20,1,640]{2,1,0:T(1,128)}, f32[1,1280]{1,0:T(1,128)}) custom-call(bf16[128,1280]{1,0:T(8,128)(2,1)} %bitcast.10, bf16[128,1280]{1,0:T(8,128)(2,1)} %bitcast.11, s32[1,128]{1,0:T(1,128)} %win_hbm.1, f32[1,1280]{1,0:T(1,128)} %gain_hbm.1, ...), custom_call_target="tpu_custom_call" | custom-call | tf_op jit(solution)/shard_map/pallas_call | solution.py:809
  88.2 2.0 %shard_map.102 = (bf16[128,1280]{1,0:T(8,128)(2,1)}, bf16[128,1280]{1,0:T(8,128)(2,1)}, f32[20,1,1920]{2,1,0:T(1,128)}, f32[20,1,640]{2,1,0:T(1,128)}, f32[1,20]{1,0:T(1,128)}) custom-call(bf16[128,1280]{1,0:T(8,128)(2,1)} %get-tuple-element.15.act, bf16[128,1280]{1,0:T(8,128)(2,1)} %get-tuple-element.16.gin, f32[20,1,1920]{2,1,0:T(1,128)} %get-tuple-element.17.out_q, ...), custom_call_target="tpu_custom_call" | custom-call | tf_op jit(solution)/shard_map/pallas_call | solution.py:819
